TPU v7x, 1024 devices: a whole 8x8x8 slice. The times are simulated.
1024 devices in a mesh: pipe: 8 (over y_hi, core), expert: 64 (over z, x), dp: 2 (over y_lo).
Axes of the slice: x: 8, y: 8 (y_hi: 4, y_lo: 2; y = y_hi * 2 + y_lo), z: 8, core: 2. Of those that a mesh axis runs over, the one named last changes fastest.
Arguments:
- tokens: bfloat16 [2048, 4096], P(('expert', 'dp'), 'pipe'), may hold values from -6 to 6
- cotangent: bfloat16 [2048, 4096], P(('expert', 'dp'), 'pipe'), may hold values from -1.5 to 1.5
- routes: int32 [2048, 8], P(('expert', 'dp')), may hold values from 0 to 63, all different within a row; in each aligned block of 16 rows (0 to 15, 16 to 31, ...) at most 3 rows name the same one
- gates: float32 [2048, 8], P(('expert', 'dp')), may hold values from 0.1 to 1
- w_gate: bfloat16 [64, 4096, 1024], P('expert', 'pipe'), may hold values from -0.09375 to 0.09375
- w_up: bfloat16 [64, 4096, 1024], P('expert', 'pipe'), may hold values from -0.09375 to 0.09375
- w_down: bfloat16 [64, 1024, 4096], P('expert', None, 'pipe'), may hold values from -0.1875 to 0.1875
Outputs:
- mixed: bfloat16 [2048, 4096], P(('expert', 'dp'), 'pipe')
- token_grad: bfloat16 [2048, 4096], P(('expert', 'dp'), 'pipe')
- grad_gate: bfloat16 [64, 4096, 1024], P('expert', 'pipe', 'dp')
- grad_up: bfloat16 [64, 4096, 1024], P('expert', 'pipe', 'dp')
- grad_down: bfloat16 [64, 1024, 4096], P('expert', 'dp', 'pipe')
Inputs may be any that keep to these rules, and one draw needn't show every extreme that they name: `routes`: each token names 8 different experts. Within the 16 rows of one device no expert is named more than 3 times, a bound that some block reaches.
All inputs are finite; a program needn't handle non-finite values.
Results may differ from a plain program's by a relative error of at most 0.0065.
Values may be sent and summed in bfloat16 or wider, within the bound.
A program may use at most 32 MiB of HBM per device.

v0:
```python
import jax
import jax.numpy as jnp
from jax import lax
from jax.sharding import PartitionSpec as P


def silu_parts(value):
    sig = jax.nn.sigmoid(value)
    return (value * sig, sig * (1.0 + value * (1.0 - sig)))


def contract_rows(left, right):
    return lax.dot_general(
        left, right, (((0,), (0,)), ((), ())), preferred_element_type=jnp.float32
    )


def contract_cols(left, right):
    return lax.dot_general(
        left, right, (((1,), (1,)), ((), ())), preferred_element_type=jnp.float32
    )


def on_device(tokens, cotangent, routes, gates, w_gate, w_up, w_down):
    tok_rows, piece = tokens.shape
    top = routes.shape[1]
    experts = lax.axis_size("expert")
    cap = max(2, 3 * tok_rows * top // (2 * experts))
    slots = experts * cap
    flat = routes.reshape(-1)
    onehot = (flat[:, None] == jnp.arange(experts, dtype=jnp.int32)[None, :]).astype(jnp.int32)
    before = jnp.sum((jnp.cumsum(onehot, axis=0) - onehot) * onehot, axis=1)
    slot_of = flat * cap + before
    place = (slot_of[:, None] == jnp.arange(slots, dtype=jnp.int32)[None, :]).astype(jnp.float32)
    owner = jnp.arange(tok_rows * top, dtype=jnp.int32) // top
    tokmat = (owner[:, None] == jnp.arange(tok_rows, dtype=jnp.int32)[None, :]).astype(jnp.float32)
    dispatch = lax.dot_general(
        place, tokmat, (((0,), (0,)), ((), ())), precision=lax.Precision.HIGHEST
    ).astype(jnp.bfloat16)
    gflat = gates.reshape(-1)
    weighted = (gflat[:, None] * jnp.repeat(cotangent, top, axis=0).astype(jnp.float32)).astype(
        jnp.bfloat16
    )
    send_x = jnp.dot(dispatch, tokens, preferred_element_type=jnp.float32).astype(jnp.bfloat16)
    send_do = contract_rows(place.astype(jnp.bfloat16), weighted).astype(jnp.bfloat16)
    got_x, got_do = (
        lax.all_to_all(
            send_x.reshape(experts, cap, piece), "expert", split_axis=0, concat_axis=0, tiled=True
        ),
        lax.all_to_all(
            send_do.reshape(experts, cap, piece), "expert", split_axis=0, concat_axis=0, tiled=True
        ),
    )
    rows_x = got_x.reshape(slots, piece)
    rows_do = got_do.reshape(slots, piece)
    w_g = w_gate[0]
    w_u = w_up[0]
    w_d = w_down[0]
    gate_pre, up_pre = lax.psum(
        (
            jnp.dot(rows_x, w_g, preferred_element_type=jnp.float32),
            jnp.dot(rows_x, w_u, preferred_element_type=jnp.float32),
        ),
        "pipe",
    )
    act, slope = silu_parts(gate_pre)
    hidden = (act * up_pre).astype(jnp.bfloat16)
    expert_out = jnp.dot(hidden, w_d, preferred_element_type=jnp.float32).astype(jnp.bfloat16)
    back_out = lax.all_to_all(
        expert_out.reshape(experts, cap, piece), "expert", split_axis=0, concat_axis=0, tiled=True
    )
    hidden_grad = lax.psum(contract_cols(rows_do, w_d), "pipe")
    gate_grad = (hidden_grad * up_pre * slope).astype(jnp.bfloat16)
    up_grad = (hidden_grad * act).astype(jnp.bfloat16)
    row_grad = (contract_cols(gate_grad, w_g) + contract_cols(up_grad, w_u)).astype(jnp.bfloat16)
    part_g = contract_rows(rows_x, gate_grad)
    part_u = contract_rows(rows_x, up_grad)
    part_d = contract_rows(hidden, rows_do)
    sum_g, sum_u, sum_d = (
        lax.psum_scatter(part_g.astype(jnp.bfloat16), "dp", scatter_dimension=1, tiled=True).astype(
            jnp.float32
        ),
        lax.psum_scatter(part_u.astype(jnp.bfloat16), "dp", scatter_dimension=1, tiled=True).astype(
            jnp.float32
        ),
        lax.psum_scatter(part_d.astype(jnp.bfloat16), "dp", scatter_dimension=0, tiled=True).astype(
            jnp.float32
        ),
    )
    back_grad = lax.all_to_all(
        row_grad.reshape(experts, cap, piece), "expert", split_axis=0, concat_axis=0, tiled=True
    )
    combine = lax.dot_general(
        tokmat, place * gflat[:, None], (((0,), (0,)), ((), ())), precision=lax.Precision.HIGHEST
    )
    mixed = jnp.dot(
        combine, back_out.reshape(slots, piece).astype(jnp.float32), precision=lax.Precision.HIGHEST
    ).astype(jnp.bfloat16)
    token_grad = contract_rows(dispatch, back_grad.reshape(slots, piece)).astype(jnp.bfloat16)
    return (
        mixed,
        token_grad,
        sum_g.astype(jnp.bfloat16)[None],
        sum_u.astype(jnp.bfloat16)[None],
        sum_d.astype(jnp.bfloat16)[None],
    )


def solution(mesh):
    in_specs = (
        P(("expert", "dp"), "pipe"),
        P(("expert", "dp"), "pipe"),
        P(("expert", "dp"), None),
        P(("expert", "dp"), None),
        P("expert", "pipe", None),
        P("expert", "pipe", None),
        P("expert", None, "pipe"),
    )
    out_specs = (
        P(("expert", "dp"), "pipe"),
        P(("expert", "dp"), "pipe"),
        P("expert", "pipe", "dp"),
        P("expert", "pipe", "dp"),
        P("expert", "dp", "pipe"),
    )
    return jax.shard_map(
        on_device, mesh=mesh, in_specs=in_specs, out_specs=out_specs, check_vma=False
    )
```

profile of v0, /device:TPU:1, one launch (start us, length us, event | category | flops | bytes accessed | tf_op | source)
XLA Modules:
  0.0 277.9 jit_solution(9194448051168922313)
XLA Ops:
  7.2 0.8 copy.14
  8.0 0.1 reshape.62
  8.1 0.1 fusion.23
  8.2 0.2 reduce_window_sum.11
  8.4 0.2 select_reduce_fusion
  8.6 0.2 convolution_convert_fusion.8
  8.9 0.9 convolution_convert_fusion.3
  9.8 0.8 reshape.63
  10.6 23.3 %all-to-all-start = ((bf16[64,3,512]{2,1,0:T(4,128)(2,1)}), bf16[64,3,512]{2,1,0:T(4,128)(2,1)S(1)}, u32[]{:S(2)}, u32[]{:S(2)}) async-start(bf16[64,3,512]{2,1,0:T(4,128)(2,1)} %reshape.63), calls=%async_computation | async-start | bytes 524288 | tf_op jit(solution)/shard_map/all_to_all | solution.py:47
  34.0 0.1 copy.15
  34.0 0.1 mul.52
  34.1 0.3 convolution_convert_fusion.4
  34.4 0.8 reshape.67
  35.3 11.3 %all-to-all-done = bf16[64,3,512]{2,1,0:T(4,128)(2,1)S(1)} async-done(((bf16[64,3,512]{2,1,0:T(4,128)(2,1)}), bf16[64,3,512]{2,1,0:T(4,128)(2,1)S(1)}, u32[]{:S(2)}, u32[]{:S(2)}) %all-to-all-start) | async-done | bytes 196640 | tf_op jit(solution)/shard_map/all_to_all | solution.py:47
  46.6 6.1 %all-to-all-start.2 = ((bf16[64,3,512]{2,1,0:T(4,128)(2,1)}), bf16[64,3,512]{2,1,0:T(4,128)(2,1)}, u32[]{:S(2)}, u32[]{:S(2)}) async-start(bf16[64,3,512]{2,1,0:T(4,128)(2,1)} %reshape.67), calls=%async_computation.2 | async-start | bytes 524288 | tf_op jit(solution)/shard_map/all_to_all | solution.py:50
  52.7 0.0 all-reduce.3.cloned.1.call-start
  52.7 0.2 reshape.64
  52.9 1.3 fusion.5
  54.2 1.3 fusion.9
  55.5 9.6 %all-to-all-done.2 = bf16[64,3,512]{2,1,0:T(4,128)(2,1)} async-done(((bf16[64,3,512]{2,1,0:T(4,128)(2,1)}), bf16[64,3,512]{2,1,0:T(4,128)(2,1)}, u32[]{:S(2)}, u32[]{:S(2)}) %all-to-all-start.2) | async-done | bytes 196640 | tf_op jit(solution)/shard_map/all_to_all | solution.py:50
  65.1 1.1 reshape.68
  66.2 1.4 fusion.1
  67.6 0.0 reduce-scatter.8.cloned.1.call-start
  67.7 95.2 %all-reduce.3.cloned.1.call-done = (f32[192,1024]{1,0:T(8,128)}, f32[192,1024]{1,0:T(8,128)}, f32[192,1024]{1,0:T(8,128)}) async-done(((f32[192,1024]{1,0:T(8,128)}, f32[192,1024]{1,0:T(8,128)}, f32[192,1024]{1,0:T(8,128)}), (f32[192,1024]{1,0:T(8,128)}, f32[192,1024]{1,0:T(8,128)}, f32[192,1024]{1,0:T(8,128)})) %all-reduce.3.cloned.1.call-update) | async-done | bytes 2359312 | tf_op jit(solution)/shard_map/psum | solution.py:59
  162.9 3.0 %multiply_convert_fusion = (bf16[192,1024]{1,0:T(8,128)(2,1)}, bf16[192,1024]{1,0:T(8,128)(2,1)}, bf16[192,1024]{1,0:T(8,128)(2,1)S(1)}) fusion(f32[192,1024]{1,0:T(8,128)} %get-tuple-element.7, f32[192,1024]{1,0:T(8,128)} %get-tuple-element.6, f32[192,1024]{1,0:T(8,128)} %get-tuple-element.5), kind=kLoop, calls=%fused_computation.21 | loop fusion | flops 2949120 | bytes 3538944 | tf_op jit(solution)/shard_map/convert_element_type | solution.py:74
  165.9 0.7 copy-done.4
  166.6 1.4 convolution_convert_fusion
  168.1 0.0 reduce-scatter.4.cloned.1.call-start
  168.2 2.5 convolution_convert_fusion.2
  170.7 2.5 convolution_convert_fusion.1
  173.2 1.0 copy-done.3
  174.2 0.5 fusion.7
  174.7 0.5 copy-done.6
  175.2 1.2 fusion
  176.3 1.7 reshape.69
  178.1 13.1 %all-to-all-start.3 = ((bf16[64,3,512]{2,1,0:T(4,128)(2,1)}), bf16[64,3,512]{2,1,0:T(4,128)(2,1)S(1)}, u32[]{:S(2)}, u32[]{:S(2)}) async-start(bf16[64,3,512]{2,1,0:T(4,128)(2,1)} %reshape.69), calls=%async_computation.3 | async-start | bytes 524288 | tf_op jit(solution)/shard_map/all_to_all | solution.py:90
  191.2 0.4 convolution_convert_fusion.5
  191.5 0.8 reshape.65
  192.4 11.3 %all-to-all-done.3 = bf16[64,3,512]{2,1,0:T(4,128)(2,1)S(1)} async-done(((bf16[64,3,512]{2,1,0:T(4,128)(2,1)}), bf16[64,3,512]{2,1,0:T(4,128)(2,1)S(1)}, u32[]{:S(2)}, u32[]{:S(2)}) %all-to-all-start.3) | async-done | bytes 196640 | tf_op jit(solution)/shard_map/all_to_all | solution.py:90
  203.6 5.2 %all-to-all-start.1 = ((bf16[64,3,512]{2,1,0:T(4,128)(2,1)}), bf16[64,3,512]{2,1,0:T(4,128)(2,1)S(1)}, u32[]{:S(2)}, u32[]{:S(2)}) async-start(bf16[64,3,512]{2,1,0:T(4,128)(2,1)} %reshape.65), calls=%async_computation.1 | async-start | bytes 524288 | tf_op jit(solution)/shard_map/all_to_all | solution.py:69
  208.9 0.3 fusion.16
  209.1 0.2 reshape.70
  209.3 12.1 %all-to-all-done.1 = bf16[64,3,512]{2,1,0:T(4,128)(2,1)S(1)} async-done(((bf16[64,3,512]{2,1,0:T(4,128)(2,1)}), bf16[64,3,512]{2,1,0:T(4,128)(2,1)S(1)}, u32[]{:S(2)}, u32[]{:S(2)}) %all-to-all-start.1) | async-done | bytes 196640 | tf_op jit(solution)/shard_map/all_to_all | solution.py:69
  221.4 0.2 reshape.66
  221.6 0.7 convolution_convert_fusion.6
  222.4 0.8 convolution_convert_fusion.7
  223.2 12.5 %reduce-scatter.4.cloned.1.call-done = bf16[512,512]{1,0:T(8,128)(2,1)} async-done(((bf16[512,1024]{1,0:T(8,128)(2,1)}), bf16[512,512]{1,0:T(8,128)(2,1)}) %reduce-scatter.4.cloned.1.call-update) | async-done | bytes 524304 | tf_op jit(solution)/shard_map/reduce_scatter | solution.py:80
  235.7 35.7 %reduce-scatter.6.cloned.1.call-done = bf16[512,512]{1,0:T(8,128)(2,1)} async-done(((bf16[512,1024]{1,0:T(8,128)(2,1)}), bf16[512,512]{1,0:T(8,128)(2,1)}) %reduce-scatter.6.cloned.1.call-update) | async-done | bytes 524304 | tf_op jit(solution)/shard_map/reduce_scatter | solution.py:83
  (27 shorter events, 0.2 us)
Async XLA Ops:
  7.2 47.0 %copy-start = (bf16[1,512,1024]{2,1,0:T(8,128)(2,1)S(1)}, bf16[1,512,1024]{2,1,0:T(8,128)(2,1)}, u32[]{:S(2)}) copy-start(bf16[1,512,1024]{2,1,0:T(8,128)(2,1)} %param.11) | copy-start | bytes 3145732
  7.2 26.8 %copy-start.8 = (f32[16,8]{0,1:T(8,128)S(1)}, f32[16,8]{0,1:T(8,128)}, u32[]{:S(2)}) copy-start(f32[16,8]{0,1:T(8,128)} %param.10) | copy-start | bytes 1540
  7.2 26.9 %copy-start.7 = (bf16[16,512]{1,0:T(8,128)(2,1)S(1)}, bf16[16,512]{1,0:T(8,128)(2,1)}, u32[]{:S(2)}) copy-start(bf16[16,512]{1,0:T(8,128)(2,1)} %param.8) | copy-start | bytes 49156
  8.6 25.3 %copy-start.9 = (s32[128]{0:T(128)}, s32[128]{0:T(128)S(1)}, u32[]{:S(2)}) copy-start(s32[128]{0:T(128)S(1)} %get-tuple-element.11) | copy-start | bytes 1540
  10.6 42.3 %copy-start.1 = (bf16[1,512,1024]{2,1,0:T(8,128)(2,1)S(1)}, bf16[1,512,1024]{2,1,0:T(8,128)(2,1)}, u32[]{:S(2)}) copy-start(bf16[1,512,1024]{2,1,0:T(8,128)(2,1)} %param.12) | copy-start | bytes 3145732
  10.6 36.0 %all-to-all-start = ((bf16[64,3,512]{2,1,0:T(4,128)(2,1)}), bf16[64,3,512]{2,1,0:T(4,128)(2,1)S(1)}, u32[]{:S(2)}, u32[]{:S(2)}) async-start(bf16[64,3,512]{2,1,0:T(4,128)(2,1)} %reshape.63), calls=%async_computation | async-start | bytes 524288 | tf_op jit(solution)/shard_map/all_to_all | solution.py:47
  46.6 18.5 %all-to-all-start.2 = ((bf16[64,3,512]{2,1,0:T(4,128)(2,1)}), bf16[64,3,512]{2,1,0:T(4,128)(2,1)}, u32[]{:S(2)}, u32[]{:S(2)}) async-start(bf16[64,3,512]{2,1,0:T(4,128)(2,1)} %reshape.67), calls=%async_computation.2 | async-start | bytes 524288 | tf_op jit(solution)/shard_map/all_to_all | solution.py:50
  52.7 110.2 %all-reduce.3.cloned.1.call-start = ((), (), s32[]{:S(2)}) async-start(), calls=%async_computation.10 | async-start | bytes 4718592 | tf_op jit(solution)/shard_map/psum | solution.py:59
  54.2 12.0 %copy-start.2 = (bf16[1,1024,512]{2,1,0:T(8,128)(2,1)S(1)}, bf16[1,1024,512]{2,1,0:T(8,128)(2,1)}, u32[]{:S(2)}) copy-start(bf16[1,1024,512]{2,1,0:T(8,128)(2,1)} %param.13) | copy-start | bytes 3145732
  67.6 155.5 %reduce-scatter.8.cloned.1.call-start = ((), (), s32[]{:S(2)}) async-start(), calls=%async_computation.9 | async-start | bytes 1572864 | tf_op jit(solution)/shard_map/reduce_scatter | solution.py:86
  165.9 0.7 copy-start.4
  168.1 67.6 %reduce-scatter.4.cloned.1.call-start = ((), (), s32[]{:S(2)}) async-start(), calls=%async_computation.7 | async-start | bytes 1572864 | tf_op jit(solution)/shard_map/reduce_scatter | solution.py:80
  170.6 100.7 %reduce-scatter.6.cloned.1.call-start = ((), (), s32[]{:S(2)}) async-start(), calls=%async_computation.8 | async-start | bytes 1572864 | tf_op jit(solution)/shard_map/reduce_scatter | solution.py:83
  173.2 1.0 copy-start.3
  174.2 1.0 copy-start.6
  175.1 16.0 %copy-start.5 = (bf16[192,1024]{1,0:T(8,128)(2,1)S(1)}, bf16[192,1024]{1,0:T(8,128)(2,1)}, u32[]{:S(2)}) copy-start(bf16[192,1024]{1,0:T(8,128)(2,1)} %copy-done.4) | copy-start | bytes 1179652
  178.1 25.6 %all-to-all-start.3 = ((bf16[64,3,512]{2,1,0:T(4,128)(2,1)}), bf16[64,3,512]{2,1,0:T(4,128)(2,1)S(1)}, u32[]{:S(2)}, u32[]{:S(2)}) async-start(bf16[64,3,512]{2,1,0:T(4,128)(2,1)} %reshape.69), calls=%async_computation.3 | async-start | bytes 524288 | tf_op jit(solution)/shard_map/all_to_all | solution.py:90
  191.1 17.7 %copy-start.10 = (s32[128]{0:T(128)S(1)}, s32[128]{0:T(128)}, u32[]{:S(2)}) copy-start(s32[128]{0:T(128)} %copy-done.9) | copy-start | bytes 1540
  203.6 17.8 %all-to-all-start.1 = ((bf16[64,3,512]{2,1,0:T(4,128)(2,1)}), bf16[64,3,512]{2,1,0:T(4,128)(2,1)S(1)}, u32[]{:S(2)}, u32[]{:S(2)}) async-start(bf16[64,3,512]{2,1,0:T(4,128)(2,1)} %reshape.65), calls=%async_computation.1 | async-start | bytes 524288 | tf_op jit(solution)/shard_map/all_to_all | solution.py:69
Sparse Core Ops, SparseCore 0:
  67.7 95.0 all-reduce.2
  168.2 31.1 reduce-scatter.7
  203.8 31.8 reduce-scatter.3
  239.5 31.8 reduce-scatter.5
where the time goes:
time: 279 us; the launch traced here: 278 us
  waiting for transfers between devices  188 us (67%)
  starting transfers between devices  47.8 us (17%)
  matrix products  15.7 us (6%)
  between operations  14 us (5%)
  local copies, waits for them, and re-layouts  9.15 us (3%)
  other arithmetic  3.48 us (1%)
    psum x1, waiting for transfers between devices, on_device(): lax.psum((jnp.dot(rows_x, w_g, preferred_element_type=jnp.float32), jnp.d...  95.2 us
    reduce_scatter x1, waiting for transfers between devices, on_device(): lax.psum_scatter(part_u.astype(jnp.bfloat16), 'dp', scatter_dimension=1,...  35.7 us
    all_to_all x1, starting transfers between devices, on_device(): lax.all_to_all(send_x.reshape(experts, cap, piece), 'expert', split_axis=...  23.3 us
    all_to_all x1, starting transfers between devices, on_device(): lax.all_to_all(row_grad.reshape(experts, cap, piece), 'expert', split_axi...  13.1 us
    reduce_scatter x1, waiting for transfers between devices, on_device(): lax.psum_scatter(part_g.astype(jnp.bfloat16), 'dp', scatter_dimension=1,...  12.5 us
    all_to_all x1, waiting for transfers between devices, on_device(): lax.all_to_all(expert_out.reshape(experts, cap, piece), 'expert', split_a...  12.1 us
    all_to_all x1, waiting for transfers between devices, on_device(): lax.all_to_all(send_x.reshape(experts, cap, piece), 'expert', split_axis=...  11.3 us
    all_to_all x1, waiting for transfers between devices, on_device(): lax.all_to_all(row_grad.reshape(experts, cap, piece), 'expert', split_axi...  11.3 us
  transfers between devices with their start and end apart: 8, of which 7 were waited for; matrix products, arithmetic and copies ran while one was open for 6% of the time, Pallas kernels for 0%

commit v1 on v0

v1 whole, which is shorter than its diff:
```python
import functools

import jax
import jax.numpy as jnp
from jax import lax
from jax.experimental import pallas as pl
from jax.experimental.pallas import tpu as pltpu
from jax.sharding import PartitionSpec as P

CAP = 3
CHIPS = 4
MESH = pl.DeviceIdType.MESH
BF16, F32 = jnp.bfloat16, jnp.float32


def dot(left, right):
    return lax.dot_general(left, right, (((1,), (0,)), ((), ())), preferred_element_type=F32)


def dot_rows(left, right):
    return lax.dot_general(left, right, (((0,), (0,)), ((), ())), preferred_element_type=F32)


def dot_cols(left, right):
    return lax.dot_general(left, right, (((1,), (1,)), ((), ())), preferred_element_type=F32)


def silu_parts(value):
    sig = 1.0 / (1.0 + jnp.exp(-value))
    return value * sig, sig * (1.0 + value * (1.0 - sig))


def iota(shape, dim):
    return lax.broadcasted_iota(jnp.int32, shape, dim)


def kernel(
    side, tok_ref, cot_ref, routes_ref, gates_ref, wg_hbm, wu_hbm, wd_hbm,
    mixed_ref, grad_ref, gg_ref, gu_ref, gd_ref,
    wg, wu, wd, tokbuf, metabuf, cmat, perm, send2, recv2, x_ref, do_ref, pair_send, pair_recv, mine,
    far_send, far_recv, imm_send, imm_recv, sum_send, sum_recv, act, send3, recv3, send4, recv4,
    w_sem, s1, r1, s1m, r1m, s2, r2, sp, rp, sy, ry, s5, r5, s3, r3, s4, r4,
):
    toks, piece = tok_ref.shape
    top = routes_ref.shape[1]
    lanes = side * toks
    block = side * CAP
    rows = 2 * side * block
    chunk = rows // (2 * CHIPS)
    half = wg.shape[1] // 2

    p, e, d = lax.axis_index("pipe"), lax.axis_index("expert"), lax.axis_index("dp")
    c, j = lax.rem(p, 2), lax.div(p, 2)
    hi, lo = lax.div(e, side), lax.rem(e, side)
    a, b = hi * (1 - c) + lo * c, lo * (1 - c) + hi * c
    sa, sb = side * (1 - c) + c, (1 - c) + side * c
    up, dn, far = lax.rem(j + 1, CHIPS), lax.rem(j + CHIPS - 1, CHIPS), lax.rem(j + 2, CHIPS)
    sib_dev = (2 * j + 1 - c, e, d)
    up_dev = (2 * up + c, e, d)
    dn_dev = (2 * dn + c, e, d)

    def a_dev(i):
        return (p, lax.rem(a + i, side) * sa + b * sb, d)

    def b_dev(i, dd):
        return (p, a * sa + lax.rem(b + i, side) * sb, lax.rem(d + dd, 2))

    b_peers = [(i, dd) for dd in range(2) for i in range(side) if i or dd]

    barrier = pltpu.get_barrier_semaphore()
    peers = [a_dev(i) for i in range(1, side)] + [b_dev(i, dd) for i, dd in b_peers]
    peers += [sib_dev, up_dev, dn_dev]
    for dev in peers:
        pl.semaphore_signal(barrier, inc=1, device_id=dev, device_id_type=MESH)

    width = wg.shape[1]
    off = pl.multiple_of(d * width, width)
    loads = [
        pltpu.make_async_copy(wg_hbm.at[0, :, pl.ds(off, width)], wg, w_sem.at[0]),
        pltpu.make_async_copy(wu_hbm.at[0, :, pl.ds(off, width)], wu, w_sem.at[1]),
        pltpu.make_async_copy(wd_hbm.at[0, pl.ds(off, width), :], wd, w_sem.at[2]),
    ]
    for load in loads:
        load.start()

    started = []

    def send(src, dst, ssem, rsem, dev):
        copy = pltpu.make_async_remote_copy(
            src_ref=src, dst_ref=dst, send_sem=ssem, recv_sem=rsem, device_id=dev, device_id_type=MESH
        )
        copy.start()
        started.append(copy)
        return copy

    tokbuf[a, 0:toks, :] = tok_ref[...]
    tokbuf[a, toks:, :] = cot_ref[...]
    lane = iota((toks, lanes), 1)
    own = (lax.rem(lane, toks) == iota((toks, lanes), 0)) & (lax.div(lane, toks) == a)
    meta = []
    for values in (routes_ref[...].astype(F32), gates_ref[...]):
        for k in range(top):
            spread = jnp.broadcast_to(values[:, k : k + 1], (toks, lanes))
            meta.append(jnp.sum(jnp.where(own, spread, 0.0), axis=0, keepdims=True))
    metabuf[a] = jnp.concatenate(meta, axis=0)

    size = 2 * side * block
    to, frm = iota((size, size), 0), iota((size, size), 1)
    to_kind, to = lax.div(to, side * block), lax.rem(to, side * block)
    to_x, to_slot, to_z = lax.div(to, block), lax.div(lax.rem(to, block), side), lax.rem(to, side)
    frm_b, frm = lax.div(frm, 2 * block), lax.rem(frm, 2 * block)
    frm_kind, frm = lax.div(frm, block), lax.rem(frm, block)
    frm_slot, frm_a = lax.div(frm, side), lax.rem(frm, side)
    same = (to_kind == frm_kind) & (to_slot == frm_slot)
    same = same & (frm_b == to_x * (1 - c) + to_z * c) & (frm_a == to_z * (1 - c) + to_x * c)
    perm[...] = jnp.where(same, 1.0, 0.0).astype(BF16)

    pl.semaphore_wait(barrier, len(peers))

    gather = []
    for i in range(1, side):
        gather.append(send(metabuf.at[a], metabuf.at[a], s1m.at[i], r1m.at[i], a_dev(i)))
    for i in range(1, side):
        gather.append(send(tokbuf.at[a], tokbuf.at[a], s1.at[i], r1.at[i], a_dev(i)))
    for copy in gather[: side - 1]:
        copy.wait_recv()

    total = metabuf[0]
    for i in range(1, side):
        total = total + metabuf[i]
    routes, gates = total[:top], total[top:]
    named, weights = [], []
    for i in range(side):
        hit = routes == (a * sa + i * sb).astype(F32)
        named.append(jnp.sum(jnp.where(hit, 1.0, 0.0), axis=0, keepdims=True))
        weights.append(jnp.sum(jnp.where(hit, gates, 0.0), axis=0, keepdims=True))
    first, second = iota((lanes, lanes), 0), iota((lanes, lanes), 1)
    earlier = (lax.div(first, toks) == lax.div(second, toks)) & (first < second)
    before = dot(
        jnp.concatenate(named, axis=0).astype(BF16), jnp.where(earlier, 1.0, 0.0).astype(BF16)
    )
    slot, source = iota((block, lanes), 0), iota((block, lanes), 1)
    here = lax.rem(slot, side) == lax.div(source, toks)
    slot = lax.div(slot, side).astype(F32)
    picks, scales = [], []
    empty = jnp.zeros((block, lanes), F32)
    for i in range(side):
        pick = jnp.where(here & (before[i : i + 1] == slot) & (named[i] > 0.5), 1.0, 0.0)
        scaled = pick * weights[i]
        picks.append(pick)
        scales.append(jnp.sum(scaled, axis=1, keepdims=True))
        high = scaled.astype(BF16).astype(F32)
        low = scaled - high
        wide = jnp.concatenate(
            [
                jnp.concatenate([high, low, empty], axis=1),
                jnp.concatenate([empty, empty, pick], axis=1),
            ],
            axis=0,
        )
        cmat[2 * block * i : 2 * block * (i + 1), :] = wide.astype(BF16)
    place = jnp.concatenate(picks, axis=0).astype(BF16)
    scale = jnp.concatenate(scales, axis=0)

    for copy in gather[side - 1 :]:
        copy.wait_recv()
    xr = dot(place, tokbuf[:, 0:toks, :].reshape(lanes, piece))
    dr = dot(place, tokbuf[:, toks:, :].reshape(lanes, piece)) * scale
    for i in range(side):
        part = slice(block * i, block * (i + 1))
        send2[i] = jnp.concatenate([xr[part], dr[part]], axis=0).astype(BF16)
    copies = []
    for i, dd in b_peers:
        k = dd * side + i
        copies.append(send(send2.at[lax.rem(b + i, side)], recv2.at[d, b], s2.at[k], r2.at[k], b_dev(i, dd)))
    recv2[d, b] = send2[b]
    for load in loads:
        load.wait()
    for copy in copies:
        copy.wait_recv()

    for g in range(2):
        sorted_rows = dot(perm[...], recv2[g].reshape(2 * side * block, piece)).astype(BF16)
        x_ref[g * side * block : (g + 1) * side * block, :] = sorted_rows[: side * block]
        do_ref[g * side * block : (g + 1) * side * block, :] = sorted_rows[side * block :]

    def rows_of(ref, core):
        return jnp.concatenate(
            [ref[pl.ds(pl.multiple_of((2 * k + core) * chunk, chunk), chunk), :] for k in range(CHIPS)], axis=0
        )

    def partials(core, out, cast, after):
        xs, ds = rows_of(x_ref, core), rows_of(do_ref, core)
        for h in range(2):
            cols = slice(h * half, (h + 1) * half)
            for q, value in enumerate((dot(xs, wg[:, cols]), dot(xs, wu[:, cols]), dot_cols(ds, wd[cols, :]))):
                for k in range(CHIPS):
                    out[h, k, q * chunk : (q + 1) * chunk, :] = value[k * chunk : (k + 1) * chunk].astype(cast)
            after(h)

    pair = []
    partials(
        1 - c, pair_send, BF16,
        lambda h: pair.append(send(pair_send.at[h], pair_recv.at[h], sp.at[h], rp.at[h], sib_dev)),
    )
    partials(c, mine, F32, lambda h: None)

    def chip_sum(h, k):
        return mine[h, k] + pair_recv[h, k].astype(F32)

    ring = ((up, up_dev, dn, dn_dev), (dn, dn_dev, up, up_dev))
    fars, imms, sums = [], [], []
    for h in range(2):
        on, on_dev, back, back_dev = ring[h]
        pair[h].wait_recv()
        far_send[h] = chip_sum(h, far).astype(BF16)
        fars.append(send(far_send.at[h], far_recv.at[h], sy.at[h], ry.at[h], on_dev))
        imm_send[h] = chip_sum(h, back).astype(BF16)
        imms.append(send(imm_send.at[h], imm_recv.at[h], sy.at[2 + h], ry.at[2 + h], back_dev))
    for h in range(2):
        on, on_dev, back, back_dev = ring[h]
        fars[h].wait_recv()
        sum_send[h] = (chip_sum(h, on) + far_recv[h].astype(F32)).astype(BF16)
        sums.append(send(sum_send.at[h], sum_recv.at[h], sy.at[4 + h], ry.at[4 + h], on_dev))

    ups, dns, sibs = [], [], []
    for h in range(2):
        imms[h].wait_recv()
        sums[h].wait_recv()
        pre = chip_sum(h, j) + imm_recv[h].astype(F32) + sum_recv[h].astype(F32)
        gate, upv, hid_grad = pre[:chunk], pre[chunk : 2 * chunk], pre[2 * chunk :]
        silu, slope = silu_parts(gate)
        act[j, c, h, 0:chunk, :] = (silu * upv).astype(BF16)
        act[j, c, h, chunk : 2 * chunk, :] = (hid_grad * upv * slope).astype(BF16)
        act[j, c, h, 2 * chunk :, :] = (hid_grad * silu).astype(BF16)
        own_piece = act.at[j, c, h]
        ups.append(send(own_piece, own_piece, s5.at[h], r5.at[h], up_dev))
        dns.append(send(own_piece, own_piece, s5.at[2 + h], r5.at[2 + h], dn_dev))
        sibs.append(send(own_piece, own_piece, s5.at[6 + h], r5.at[6 + h], sib_dev))
    ups[0].wait_recv()
    below = act.at[dn, c, 0]
    far0 = send(below, below, s5.at[4], r5.at[4], up_dev)
    dns[1].wait_recv()
    above = act.at[up, c, 1]
    far1 = send(above, above, s5.at[5], r5.at[5], dn_dev)
    sibs.append(send(below, below, s5.at[8], r5.at[8], sib_dev))
    sibs.append(send(above, above, s5.at[9], r5.at[9], sib_dev))
    ups[1].wait_recv()
    piece1 = act.at[dn, c, 1]
    sibs.append(send(piece1, piece1, s5.at[10], r5.at[10], sib_dev))
    dns[0].wait_recv()
    piece0 = act.at[up, c, 0]
    sibs.append(send(piece0, piece0, s5.at[11], r5.at[11], sib_dev))
    for h, copy in enumerate((far0, far1)):
        copy.wait_recv()
        piece2 = act.at[far, c, h]
        sibs.append(send(piece2, piece2, s5.at[12 + h], r5.at[12 + h], sib_dev))
    for copy in sibs:
        copy.wait_recv()

    def gathered(q):
        part = slice(q * chunk, (q + 1) * chunk)
        return jnp.concatenate(
            [
                jnp.concatenate([act[k, core, 0, part, :], act[k, core, 1, part, :]], axis=1)
                for k in range(CHIPS)
                for core in range(2)
            ],
            axis=0,
        )

    hidden, gate_grad, up_grad = gathered(0), gathered(1), gathered(2)
    outs = dot(hidden, wd[...])
    row_grads = dot_cols(gate_grad, wg[...]) + dot_cols(up_grad, wu[...])
    for g in range(2):
        part = slice(g * side * block, (g + 1) * side * block)
        stacked = jnp.concatenate([outs[part], row_grads[part]], axis=0).astype(BF16)
        send3[g] = dot_rows(perm[...], stacked).astype(BF16).reshape(side, 2 * block, piece)
    copies = []
    for i, dd in b_peers:
        k = dd * side + i
        copies.append(
            send(
                send3.at[lax.rem(d + dd, 2), lax.rem(b + i, side)], recv3.at[d, b], s3.at[k], r3.at[k], b_dev(i, dd)
            )
        )
    recv3[d, b] = send3[d, b]

    gg_ref[0] = dot_rows(x_ref[...], gate_grad).astype(BF16)
    gu_ref[0] = dot_rows(x_ref[...], up_grad).astype(BF16)
    gd_ref[0] = dot_rows(hidden, do_ref[...]).astype(BF16)

    for copy in copies:
        copy.wait_recv()
    both = dot_rows(cmat[...], recv3[0].reshape(2 * side * block, piece))
    both = both + dot_rows(cmat[...], recv3[1].reshape(2 * side * block, piece))
    part_mixed = both[:lanes] + both[lanes : 2 * lanes]
    part_grad = both[2 * lanes :]
    for i in range(side):
        part = slice(i * toks, (i + 1) * toks)
        send4[i] = jnp.concatenate([part_mixed[part], part_grad[part]], axis=0).astype(BF16)
    copies = []
    for i in range(1, side):
        copies.append(send(send4.at[lax.rem(a + i, side)], recv4.at[a], s4.at[i], r4.at[i], a_dev(i)))
    recv4[a] = send4[a]
    for copy in copies:
        copy.wait_recv()
    final = recv4[0].astype(F32)
    for i in range(1, side):
        final = final + recv4[i].astype(F32)
    mixed_ref[...] = final[:toks].astype(BF16)
    grad_ref[...] = final[toks:].astype(BF16)
    for copy in started:
        copy.wait_send()


def on_device(side, tokens, cotangent, routes, gates, w_gate, w_up, w_down):
    toks, piece = tokens.shape
    top = routes.shape[1]
    width = w_gate.shape[2] // 2
    half = width // 2
    lanes = side * toks
    block = side * CAP
    rows = 2 * side * block
    chunk = rows // (2 * CHIPS)
    vmem = pl.BlockSpec(memory_space=pltpu.VMEM)
    hbm = pl.BlockSpec(memory_space=pl.ANY)
    dma = pltpu.SemaphoreType.DMA
    quarter = (2, 3 * chunk, half)
    return pl.pallas_call(
        functools.partial(kernel, side),
        out_shape=(
            jax.ShapeDtypeStruct((toks, piece), BF16),
            jax.ShapeDtypeStruct((toks, piece), BF16),
            jax.ShapeDtypeStruct((1, piece, width), BF16),
            jax.ShapeDtypeStruct((1, piece, width), BF16),
            jax.ShapeDtypeStruct((1, width, piece), BF16),
        ),
        in_specs=[vmem] * 4 + [hbm] * 3,
        out_specs=(vmem,) * 5,
        scratch_shapes=[
            pltpu.VMEM((piece, width), BF16),
            pltpu.VMEM((piece, width), BF16),
            pltpu.VMEM((width, piece), BF16),
            pltpu.VMEM((side, 2 * toks, piece), BF16),
            pltpu.VMEM((side, 2 * top, lanes), F32),
            pltpu.VMEM((2 * side * block, 3 * lanes), BF16),
            pltpu.VMEM((2 * side * block, 2 * side * block), BF16),
            pltpu.VMEM((side, 2 * block, piece), BF16),
            pltpu.VMEM((2, side, 2 * block, piece), BF16),
            pltpu.VMEM((rows, piece), BF16),
            pltpu.VMEM((rows, piece), BF16),
            pltpu.VMEM((2, CHIPS, 3 * chunk, half), BF16),
            pltpu.VMEM((2, CHIPS, 3 * chunk, half), BF16),
            pltpu.VMEM((2, CHIPS, 3 * chunk, half), F32),
            pltpu.VMEM(quarter, BF16),
            pltpu.VMEM(quarter, BF16),
            pltpu.VMEM(quarter, BF16),
            pltpu.VMEM(quarter, BF16),
            pltpu.VMEM(quarter, BF16),
            pltpu.VMEM(quarter, BF16),
            pltpu.VMEM((CHIPS, 2, 2, 3 * chunk, half), BF16),
            pltpu.VMEM((2, side, 2 * block, piece), BF16),
            pltpu.VMEM((2, side, 2 * block, piece), BF16),
            pltpu.VMEM((side, 2 * toks, piece), BF16),
            pltpu.VMEM((side, 2 * toks, piece), BF16),
            dma((3,)),
            dma((side,)), dma((side,)), dma((side,)), dma((side,)),
            dma((2 * side,)), dma((2 * side,)),
            dma((2,)), dma((2,)),
            dma((6,)), dma((6,)),
            dma((14,)), dma((14,)),
            dma((2 * side,)), dma((2 * side,)),
            dma((side,)), dma((side,)),
        ],
        compiler_params=pltpu.CompilerParams(
            collective_id=0, has_side_effects=True, vmem_limit_bytes=40 * 1024 * 1024
        ),
        cost_estimate=pl.CostEstimate(
            flops=16 * rows * piece * width, bytes_accessed=6 * piece * width * 2, transcendentals=0
        ),
    )(tokens, cotangent, routes, gates, w_gate, w_up, w_down)


def solution(mesh):
    experts = mesh.shape["expert"]
    side = next(s for s in range(1, experts + 1) if s * s == experts)
    in_specs = (
        P(("expert", "dp"), "pipe"),
        P(("expert", "dp"), "pipe"),
        P(("expert", "dp"), None),
        P(("expert", "dp"), None),
        P("expert", "pipe", None),
        P("expert", "pipe", None),
        P("expert", None, "pipe"),
    )
    out_specs = (
        P(("expert", "dp"), "pipe"),
        P(("expert", "dp"), "pipe"),
        P("expert", "pipe", "dp"),
        P("expert", "pipe", "dp"),
        P("expert", "dp", "pipe"),
    )
    return jax.shard_map(
        functools.partial(on_device, side), mesh=mesh, in_specs=in_specs, out_specs=out_specs, check_vma=False
    )
```

time: 279 us -> 103 us (0.37)
  waiting for transfers between devices: 188 us -> 0 us
  Pallas kernels: 0 us -> 93.3 us
  starting transfers between devices: 47.8 us -> 0 us
  matrix products: 15.7 us -> 0 us
  between operations: 14 us -> 0.66 us
  other arithmetic: 3.48 us -> 0 us
    psum x1 -> x0, waiting for transfers between devices: 95.2 us -> none  [on_device(): lax.psum((jnp.dot(rows_x, w_g, preferred_element_type=jnp.float32), jnp.d...]
    pallas_call x0 -> x1, Pallas kernels: none -> 93.3 us  [on_device(): pl.pallas_call(functools.partial(kernel, side), out_shape=(jax.ShapeDtype...]
    reduce_scatter x3 -> x0, waiting for transfers between devices: 48.2 us -> none  [the longest x1 35.7 us: on_device(): lax.psum_scatter(part_u.astype(jnp.bfloat16), 'dp', scatter_dimension=1,...]
    all_to_all x4 -> x0, starting transfers between devices: 47.7 us -> none  [the longest x1 23.3 us: on_device(): lax.all_to_all(send_x.reshape(experts, cap, piece), 'expert', split_axis=...]
    all_to_all x4 -> x0, waiting for transfers between devices: 44.3 us -> none  [the longest x1 12.1 us: on_device(): lax.all_to_all(expert_out.reshape(experts, cap, piece), 'expert', split_a...]
    dot_general x15 -> x0, matrix products: 15.7 us -> none  [the longest x5 7.42 us: contract_rows(): lax.dot_general(left, right, (((0,), (0,)), ((), ())), preferred_element_...]
    reshape x9 -> x0, local copies, waits for them, and re-layouts: 5.9 us -> none  [the longest x1 1.74 us: on_device(): row_grad.reshape(experts, cap, piece)]
    unnamed x24 -> x19, local copies, waits for them, and re-layouts: 3.16 us -> 8.83 us
  transfers between devices with their start and end apart: 8 -> 0, of which waited for: 7 -> 0; matrix products, arithmetic and copies ran while one was open for 6% -> 0% of each run, Pallas kernels for 0% -> 0%
where the time goes in v1:
time: 103 us
  Pallas kernels  93.3 us (91%)
  local copies, waits for them, and re-layouts  8.83 us (9%)
    pallas_call x1, Pallas kernels, on_device(): pl.pallas_call(functools.partial(kernel, side), out_shape=(jax.ShapeDtype...  93.3 us
    unnamed x19, local copies, waits for them, and re-layouts  8.83 us

profile of v1, /device:TPU:1, one launch (start us, length us, event | category | flops | bytes accessed | tf_op | source)
XLA Modules:
  0.0 102.8 jit_solution(10204167306088966278)
XLA Ops:
  0.6 0.0 copy-start.5
  0.6 0.0 copy-start.3
  0.7 0.8 copy.12.routes_ref
  1.4 0.0 copy-done.5
  1.4 0.1 copy.13.gates_ref
  1.5 0.0 copy-done.3
  1.5 0.0 copy-start
  1.5 1.2 %copy-done = bf16[1,512,1024]{2,1,0:T(8,128)(2,1)S(1)} copy-done((bf16[1,512,1024]{2,1,0:T(8,128)(2,1)S(1)}, bf16[1,512,1024]{2,1,0:T(8,128)(2,1)}, u32[]{:S(2)}) %copy-start) | copy-done | bytes 1048600
  2.7 0.0 copy-start.1
  2.7 1.2 %copy-done.1 = bf16[1,512,1024]{2,1,0:T(8,128)(2,1)S(1)} copy-done((bf16[1,512,1024]{2,1,0:T(8,128)(2,1)S(1)}, bf16[1,512,1024]{2,1,0:T(8,128)(2,1)}, u32[]{:S(2)}) %copy-start.1) | copy-done | bytes 1048600
  3.9 0.0 copy-start.2
  4.0 1.2 %copy-done.2 = bf16[1,1024,512]{2,1,0:T(8,128)(2,1)S(1)} copy-done((bf16[1,1024,512]{2,1,0:T(8,128)(2,1)S(1)}, bf16[1,1024,512]{2,1,0:T(8,128)(2,1)}, u32[]{:S(2)}) %copy-start.2) | copy-done | bytes 1048600
  5.2 0.0 copy-start.4
  5.2 0.7 copy-done.4
  5.9 93.3 %shard_map.110 = (bf16[16,512]{1,0:T(8,128)(2,1)S(1)}, bf16[16,512]{1,0:T(8,128)(2,1)S(1)}, bf16[1,512,512]{2,1,0:T(8,128)(2,1)S(1)}, bf16[1,512,512]{2,1,0:T(8,128)(2,1)S(1)}, bf16[1,512,512]{2,1,0:T(8,128)(2,1)S(1)}) custom-call(bf16[16,512]{1,0:T(8,128)(2,1)S(1)} %copy-done.3, bf16[16,512]{1,0:T(8,128)(2,1)S(1)} %copy-done.4, ...), custom_call_target="tpu_custom_call" | custom-call | flops 1610612736 | bytes 3145728 | tf_op jit(solution)/shard_map/pallas_call | solution.py:330
  99.2 0.6 copy.19
  99.8 0.6 copy.20
  100.4 0.8 copy.21
  101.2 0.8 copy.22
  102.0 0.8 copy.23
Async XLA Ops:
  0.6 0.8 copy-start.5
  0.6 0.9 copy-start.3
  1.5 1.2 %copy-start = (bf16[1,512,1024]{2,1,0:T(8,128)(2,1)S(1)}, bf16[1,512,1024]{2,1,0:T(8,128)(2,1)}, u32[]{:S(2)}) copy-start(bf16[1,512,1024]{2,1,0:T(8,128)(2,1)} %wg_hbm.1) | copy-start | bytes 3145732
  2.7 1.2 %copy-start.1 = (bf16[1,512,1024]{2,1,0:T(8,128)(2,1)S(1)}, bf16[1,512,1024]{2,1,0:T(8,128)(2,1)}, u32[]{:S(2)}) copy-start(bf16[1,512,1024]{2,1,0:T(8,128)(2,1)} %wu_hbm.1) | copy-start | bytes 3145732
  3.9 1.2 %copy-start.2 = (bf16[1,1024,512]{2,1,0:T(8,128)(2,1)S(1)}, bf16[1,1024,512]{2,1,0:T(8,128)(2,1)}, u32[]{:S(2)}) copy-start(bf16[1,1024,512]{2,1,0:T(8,128)(2,1)} %wd_hbm.1) | copy-start | bytes 3145732
  5.2 0.7 copy-start.4

commit v2 on v1

v2 whole, which is shorter than its diff:
```python
import functools

import jax
import jax.numpy as jnp
from jax import lax
from jax.experimental import pallas as pl
from jax.experimental.pallas import tpu as pltpu
from jax.sharding import PartitionSpec as P

CAP = 3
CHIPS = 4
VMEM_LIMIT = 60 * 1024 * 1024
MESH = pl.DeviceIdType.MESH
BF16, F32 = jnp.bfloat16, jnp.float32


def dot(left, right):
    return lax.dot_general(left, right, (((1,), (0,)), ((), ())), preferred_element_type=F32)


def dot_rows(left, right):
    return lax.dot_general(left, right, (((0,), (0,)), ((), ())), preferred_element_type=F32)


def dot_cols(left, right):
    return lax.dot_general(left, right, (((1,), (1,)), ((), ())), preferred_element_type=F32)


def silu_parts(value):
    sig = 1.0 / (1.0 + jnp.exp(-value))
    return value * sig, sig * (1.0 + value * (1.0 - sig))


def iota(shape, dim):
    return lax.broadcasted_iota(jnp.int32, shape, dim)


def kernel(
    side, tok_ref, cot_ref, routes_ref, gates_ref, wg_hbm, wu_hbm, wd_hbm,
    mixed_out, grad_out, gg_out, gu_out, gd_out,
    routes_vmem, gates_vmem, mixed_ref, grad_ref, gg_ref, gu_ref, gd_ref, in_sem, out_sem, wg, wu, wd,
    tokbuf, metabuf, cmat, perm, perm_back, send2, recv2, x_ref, do_ref, pair_send, pair_recv, mine,
    far_send, far_recv, imm_send, imm_recv, sum_send, sum_recv, act, send3, recv3, send4, recv4,
    w_sem, s1, r1, s1m, r1m, s2, r2, sp, rp, sy, ry, s5, r5, s3, r3, s4, r4,
):
    toks, piece = tok_ref.shape
    top = routes_ref.shape[0]
    lanes = side * toks
    block = side * CAP
    rows = side * block
    size = 2 * rows
    width = wg.shape[1]
    cols = width // CHIPS
    part = rows // 4

    p, e, d = lax.axis_index("pipe"), lax.axis_index("expert"), lax.axis_index("dp")
    c, j = lax.rem(p, 2), lax.div(p, 2)
    hi, lo = lax.div(e, side), lax.rem(e, side)
    a, b = hi * (1 - c) + lo * c, lo * (1 - c) + hi * c
    sa, sb = side * (1 - c) + c, (1 - c) + side * c
    up, dn, far = lax.rem(j + 1, CHIPS), lax.rem(j + CHIPS - 1, CHIPS), lax.rem(j + 2, CHIPS)
    sib_dev = (2 * j + 1 - c, e, d)
    up_dev = (2 * up + c, e, d)
    dn_dev = (2 * dn + c, e, d)

    def a_dev(i):
        return (p, lax.rem(a + i, side) * sa + b * sb, d)

    def b_dev(i, s):
        return (p, a * sa + lax.rem(b + i, side) * sb, lax.rem(d + s, 2))

    b_peers = [[i for i in range(side) if i or s] for s in range(2)]

    barrier = pltpu.get_barrier_semaphore()
    peers = [a_dev(i) for i in range(1, side)] + [b_dev(i, s) for s in range(2) for i in b_peers[s]]
    peers += [sib_dev, up_dev, dn_dev]
    for dev in peers:
        pl.semaphore_signal(barrier, inc=1, device_id=dev, device_id_type=MESH)

    inputs = [
        pltpu.make_async_copy(routes_ref, routes_vmem, in_sem.at[0]),
        pltpu.make_async_copy(gates_ref, gates_vmem, in_sem.at[1]),
        pltpu.make_async_copy(tok_ref, tokbuf.at[a, pl.ds(0, toks)], in_sem.at[2]),
        pltpu.make_async_copy(cot_ref, tokbuf.at[a, pl.ds(toks, toks)], in_sem.at[3]),
    ]
    for load in inputs:
        load.start()
    off = pl.multiple_of(d * width, width)
    loads = [
        pltpu.make_async_copy(wg_hbm.at[0, :, pl.ds(off, width)], wg, w_sem.at[0]),
        pltpu.make_async_copy(wu_hbm.at[0, :, pl.ds(off, width)], wu, w_sem.at[1]),
        pltpu.make_async_copy(wd_hbm.at[0, pl.ds(off, width), :], wd, w_sem.at[2]),
    ]
    for load in loads:
        load.start()

    started = []

    def send(src, dst, ssem, rsem, dev):
        copy = pltpu.make_async_remote_copy(
            src_ref=src, dst_ref=dst, send_sem=ssem, recv_sem=rsem, device_id=dev, device_id_type=MESH
        )
        copy.start()
        started.append(copy)
        return copy

    own = lax.div(iota((2 * top, lanes), 1), toks) == a
    for load in inputs:
        load.wait()
    values = jnp.concatenate([routes_vmem[...].astype(F32), gates_vmem[...]], axis=0)
    metabuf[a] = jnp.where(own, jnp.concatenate([values] * side, axis=1), 0.0)

    pl.semaphore_wait(barrier, len(peers))

    gather = []
    for i in range(1, side):
        gather.append(send(metabuf.at[a], metabuf.at[a], s1m.at[i], r1m.at[i], a_dev(i)))
    for i in range(1, side):
        gather.append(send(tokbuf.at[a], tokbuf.at[a], s1.at[i], r1.at[i], a_dev(i)))

    def sorted_place(at):
        at_b, at = lax.div(at, 2 * block), lax.rem(at, 2 * block)
        kind, at = lax.div(at, block), lax.rem(at, block)
        slot, at_a = lax.div(at, side), lax.rem(at, side)
        at_x, at_z = at_b * (1 - c) + at_a * c, at_a * (1 - c) + at_b * c
        return kind * rows + at_x * block + slot * side + at_z

    perm[...] = jnp.where(iota((size, size), 0) == sorted_place(iota((1, size), 1)), 1.0, 0.0).astype(BF16)
    perm_back[...] = jnp.where(iota((size, size), 1) == sorted_place(iota((size, 1), 0)), 1.0, 0.0).astype(BF16)
    first, second = iota((lanes, lanes), 0), iota((lanes, lanes), 1)
    earlier = (lax.div(first, toks) == lax.div(second, toks)) & (first < second)
    earlier = jnp.where(earlier, 1.0, 0.0).astype(BF16)
    slot, source = iota((block, lanes), 0), iota((block, lanes), 1)
    here = lax.rem(slot, side) == lax.div(source, toks)
    slot = lax.div(slot, side).astype(F32)

    for copy in gather[: side - 1]:
        copy.wait_recv()

    total = metabuf[0]
    for i in range(1, side):
        total = total + metabuf[i]
    routes, gates = total[:top], total[top:]
    named, weights = [], []
    for i in range(side):
        hit = routes == (a * sa + i * sb).astype(F32)
        named.append(jnp.sum(jnp.where(hit, 1.0, 0.0), axis=0, keepdims=True))
        weights.append(jnp.sum(jnp.where(hit, gates, 0.0), axis=0, keepdims=True))
    before = dot(jnp.concatenate(named, axis=0).astype(BF16), earlier)
    picks, scales = [], []
    for i in range(side):
        pick = jnp.where(here & (before[i : i + 1] == slot) & (named[i] > 0.5), 1.0, 0.0)
        picks.append(pick)
        scales.append(jnp.sum(pick * weights[i], axis=1, keepdims=True))
    place = jnp.concatenate(picks, axis=0).astype(BF16)
    scale = jnp.concatenate(scales, axis=0)

    for copy in gather[side - 1 :]:
        copy.wait_recv()
    xr = dot(place, tokbuf[:, 0:toks, :].reshape(lanes, piece))
    dr = dot(place, tokbuf[:, toks:, :].reshape(lanes, piece)) * scale
    for i in range(side):
        at = slice(block * i, block * (i + 1))
        send2[i] = jnp.concatenate([xr[at], dr[at]], axis=0).astype(BF16)
    to_experts = [[], []]
    for s in range(2):
        for i in b_peers[s]:
            to_experts[s].append(
                send(send2.at[lax.rem(b + i, side)], recv2.at[s, b], s2.at[s, i], r2.at[s, i], b_dev(i, s))
            )
    recv2[0, b] = send2[b]

    empty = jnp.zeros((block, lanes), F32)
    wide = []
    for i in range(side):
        scaled = picks[i] * weights[i]
        high = scaled.astype(BF16).astype(F32)
        wide.append(jnp.concatenate([high, scaled - high, empty], axis=1))
        wide.append(jnp.concatenate([empty, empty, picks[i]], axis=1))
    cmat[...] = jnp.concatenate(wide, axis=0).T.astype(BF16)

    for load in loads:
        load.wait()

    pair, fars, imms, sums, ups, dns, sibs, relays = ([None, None] for _ in range(8))
    ring = ((up, up_dev, dn, dn_dev), (dn, dn_dev, up, up_dev))

    def partials(s, core, out, cast):
        at = pl.ds(pl.multiple_of(s * rows + core * 2 * part, 2 * part), 2 * part)
        xs, ds = x_ref[at, :], do_ref[at, :]
        for q, value in enumerate((dot(xs, wg[...]), dot(xs, wu[...]), dot_cols(ds, wd[...]))):
            for h in range(2):
                for k in range(CHIPS):
                    out[s, h, k, q * part : (q + 1) * part, :] = value[
                        h * part : (h + 1) * part, k * cols : (k + 1) * cols
                    ].astype(cast)

    def project(s):
        for copy in to_experts[s]:
            copy.wait_recv()
        found = dot(perm[...], recv2[s].reshape(size, piece)).astype(BF16)
        x_ref[s * rows : (s + 1) * rows, :] = found[:rows]
        do_ref[s * rows : (s + 1) * rows, :] = found[rows:]
        partials(s, 1 - c, pair_send, BF16)
        pair[s] = send(pair_send.at[s], pair_recv.at[s], sp.at[s], rp.at[s], sib_dev)
        partials(s, c, mine, F32)

    def chip_sum(s, h, k):
        return mine[s, h, k] + pair_recv[s, h, k].astype(F32)

    def scatter_start(s):
        fars[s], imms[s] = [], []
        pair[s].wait_recv()
        for h in range(2):
            far_send[s, h] = chip_sum(s, h, far).astype(BF16)
            fars[s].append(send(far_send.at[s, h], far_recv.at[s, h], sy.at[s, h], ry.at[s, h], ring[h][1]))
        for h in range(2):
            imm_send[s, h] = chip_sum(s, h, ring[h][2]).astype(BF16)
            imms[s].append(
                send(imm_send.at[s, h], imm_recv.at[s, h], sy.at[s, 2 + h], ry.at[s, 2 + h], ring[h][3])
            )

    def scatter_end(s):
        sums[s] = []
        for h in range(2):
            fars[s][h].wait_recv()
            sum_send[s, h] = (chip_sum(s, h, ring[h][0]) + far_recv[s, h].astype(F32)).astype(BF16)
            sums[s].append(
                send(sum_send.at[s, h], sum_recv.at[s, h], sy.at[s, 4 + h], ry.at[s, 4 + h], ring[h][1])
            )

    def pass_on(s, k, core, h, sem, dev):
        ref = act.at[s, k, core, h]
        return send(ref, ref, s5.at[s, sem], r5.at[s, sem], dev)

    def activate(s):
        ups[s], dns[s], sibs[s] = [], [], []
        for h in range(2):
            imms[s][h].wait_recv()
            sums[s][h].wait_recv()
            pre = chip_sum(s, h, j) + imm_recv[s, h].astype(F32) + sum_recv[s, h].astype(F32)
            gate, upv, hid_grad = pre[:part], pre[part : 2 * part], pre[2 * part :]
            silu, slope = silu_parts(gate)
            act[s, j, c, h, 0:part, :] = (silu * upv).astype(BF16)
            act[s, j, c, h, part : 2 * part, :] = (hid_grad * upv * slope).astype(BF16)
            act[s, j, c, h, 2 * part :, :] = (hid_grad * silu).astype(BF16)
            ups[s].append(pass_on(s, j, c, h, h, up_dev))
            dns[s].append(pass_on(s, j, c, h, 2 + h, dn_dev))
            sibs[s].append(pass_on(s, j, c, h, 6 + h, sib_dev))

    def relay(s):
        ups[s][0].wait_recv()
        relays[s] = [pass_on(s, dn, c, 0, 4, up_dev)]
        dns[s][1].wait_recv()
        relays[s].append(pass_on(s, up, c, 1, 5, dn_dev))
        sibs[s].append(pass_on(s, dn, c, 0, 8, sib_dev))
        sibs[s].append(pass_on(s, up, c, 1, 9, sib_dev))
        ups[s][1].wait_recv()
        sibs[s].append(pass_on(s, dn, c, 1, 10, sib_dev))
        dns[s][0].wait_recv()
        sibs[s].append(pass_on(s, up, c, 0, 11, sib_dev))

    def relay_end(s):
        for h in range(2):
            relays[s][h].wait_recv()
            sibs[s].append(pass_on(s, far, c, h, 12 + h, sib_dev))
        for copy in sibs[s]:
            copy.wait_recv()

    def gathered(s, q):
        at = slice(q * part, (q + 1) * part)
        return jnp.concatenate(
            [
                jnp.concatenate([act[s, k, core, h, at, :] for k in range(CHIPS)], axis=1)
                for core in range(2)
                for h in range(2)
            ],
            axis=0,
        )

    to_tokens = [[], []]

    def answer(s):
        outs = dot(gathered(s, 0), wd[...])
        row_grads = dot_cols(gathered(s, 1), wg[...]) + dot_cols(gathered(s, 2), wu[...])
        stacked = jnp.concatenate([outs, row_grads], axis=0).astype(BF16)
        send3[s] = dot(perm_back[...], stacked).astype(BF16).reshape(side, 2 * block, piece)
        for i in b_peers[s]:
            to_tokens[s].append(
                send(send3.at[s, lax.rem(b + i, side)], recv3.at[s, b], s3.at[s, i], r3.at[s, i], b_dev(i, s))
            )
        if s == 0:
            recv3[0, b] = send3[0, b]

    project(0)
    scatter_start(0)
    project(1)
    scatter_end(0)
    scatter_start(1)
    activate(0)
    scatter_end(1)
    relay(0)
    activate(1)
    relay_end(0)
    relay(1)
    answer(0)
    relay_end(1)
    answer(1)

    hidden, gate_grad, up_grad = (
        jnp.concatenate([gathered(0, q), gathered(1, q)], axis=0) for q in range(3)
    )
    stores = []
    for k, (ref, out, left, right) in enumerate(
        ((gg_ref, gg_out, x_ref[...], gate_grad), (gu_ref, gu_out, x_ref[...], up_grad), (gd_ref, gd_out, hidden, do_ref[...]))
    ):
        ref[...] = dot_rows(left, right).astype(BF16)
        stores.append(pltpu.make_async_copy(ref, out.at[0], out_sem.at[k]))
        stores[-1].start()

    both = None
    for s in range(2):
        for copy in to_tokens[s]:
            copy.wait_recv()
        value = dot(cmat[...], recv3[s].reshape(size, piece))
        both = value if both is None else both + value
    part_mixed = both[:lanes] + both[lanes : 2 * lanes]
    part_grad = both[2 * lanes :]
    for i in range(side):
        at = slice(i * toks, (i + 1) * toks)
        send4[i] = jnp.concatenate([part_mixed[at], part_grad[at]], axis=0).astype(BF16)
    home = []
    for i in range(1, side):
        home.append(send(send4.at[lax.rem(a + i, side)], recv4.at[a], s4.at[i], r4.at[i], a_dev(i)))
    recv4[a] = send4[a]
    for copy in home:
        copy.wait_recv()
    final = recv4[0].astype(F32)
    for i in range(1, side):
        final = final + recv4[i].astype(F32)
    mixed_ref[...] = final[:toks].astype(BF16)
    grad_ref[...] = final[toks:].astype(BF16)
    for k, (ref, out) in enumerate(((mixed_ref, mixed_out), (grad_ref, grad_out))):
        stores.append(pltpu.make_async_copy(ref, out, out_sem.at[3 + k]))
        stores[-1].start()
    for copy in stores:
        copy.wait()
    for copy in started:
        copy.wait_send()


def store(*refs):
    ins, outs, held, sems = refs[:5], refs[5:10], refs[10:15], refs[15]
    loads = [pltpu.make_async_copy(ins[i], held[i], sems.at[0, i]) for i in range(5)]
    stores = [pltpu.make_async_copy(held[i], outs[i], sems.at[1, i]) for i in range(5)]
    for load in loads:
        load.start()
    for load, copy in zip(loads, stores):
        load.wait()
        copy.start()
    for copy in stores:
        copy.wait()


def on_device(side, tokens, cotangent, routes, gates, w_gate, w_up, w_down):
    toks, piece = tokens.shape
    top = routes.shape[1]
    width = w_gate.shape[2] // 2
    lanes = side * toks
    block = side * CAP
    rows = side * block
    part = rows // 4
    hbm = pl.BlockSpec(memory_space=pltpu.MemorySpace.HBM)
    dma = pltpu.SemaphoreType.DMA
    halves = (2, 2, 3 * part, width // CHIPS)
    pieces = (2, 2, CHIPS, 3 * part, width // CHIPS)
    results = pl.pallas_call(
        functools.partial(kernel, side),
        out_shape=(
            jax.ShapeDtypeStruct((toks, piece), BF16),
            jax.ShapeDtypeStruct((toks, piece), BF16),
            jax.ShapeDtypeStruct((1, piece, width), BF16),
            jax.ShapeDtypeStruct((1, piece, width), BF16),
            jax.ShapeDtypeStruct((1, width, piece), BF16),
        ),
        in_specs=[hbm] * 7,
        out_specs=(hbm,) * 5,
        scratch_shapes=[
            pltpu.VMEM((top, toks), jnp.int32),
            pltpu.VMEM((top, toks), F32),
            pltpu.VMEM((toks, piece), BF16),
            pltpu.VMEM((toks, piece), BF16),
            pltpu.VMEM((piece, width), BF16),
            pltpu.VMEM((piece, width), BF16),
            pltpu.VMEM((width, piece), BF16),
            dma((4,)), dma((5,)),
            pltpu.VMEM((piece, width), BF16),
            pltpu.VMEM((piece, width), BF16),
            pltpu.VMEM((width, piece), BF16),
            pltpu.VMEM((side, 2 * toks, piece), BF16),
            pltpu.VMEM((side, 2 * top, lanes), F32),
            pltpu.VMEM((3 * lanes, 2 * rows), BF16),
            pltpu.VMEM((2 * rows, 2 * rows), BF16),
            pltpu.VMEM((2 * rows, 2 * rows), BF16),
            pltpu.VMEM((side, 2 * block, piece), BF16),
            pltpu.VMEM((2, side, 2 * block, piece), BF16),
            pltpu.VMEM((2 * rows, piece), BF16),
            pltpu.VMEM((2 * rows, piece), BF16),
            pltpu.VMEM(pieces, BF16),
            pltpu.VMEM(pieces, BF16),
            pltpu.VMEM(pieces, F32),
            pltpu.VMEM(halves, BF16),
            pltpu.VMEM(halves, BF16),
            pltpu.VMEM(halves, BF16),
            pltpu.VMEM(halves, BF16),
            pltpu.VMEM(halves, BF16),
            pltpu.VMEM(halves, BF16),
            pltpu.VMEM((2, CHIPS, 2, 2, 3 * part, width // CHIPS), BF16),
            pltpu.VMEM((2, side, 2 * block, piece), BF16),
            pltpu.VMEM((2, side, 2 * block, piece), BF16),
            pltpu.VMEM((side, 2 * toks, piece), BF16),
            pltpu.VMEM((side, 2 * toks, piece), BF16),
            dma((3,)),
            dma((side,)), dma((side,)), dma((side,)), dma((side,)),
            dma((2, side)), dma((2, side)),
            dma((2,)), dma((2,)),
            dma((2, 6)), dma((2, 6)),
            dma((2, 14)), dma((2, 14)),
            dma((2, side)), dma((2, side)),
            dma((side,)), dma((side,)),
        ],
        compiler_params=pltpu.CompilerParams(
            collective_id=0, has_side_effects=True, vmem_limit_bytes=VMEM_LIMIT
        ),
        cost_estimate=pl.CostEstimate(
            flops=32 * rows * piece * width, bytes_accessed=6 * piece * width * 2, transcendentals=0
        ),
    )(tokens, cotangent, routes.T, gates.T, w_gate, w_up, w_down)
    return pl.pallas_call(
        store,
        out_shape=[jax.ShapeDtypeStruct(value.shape, value.dtype) for value in results],
        in_specs=[hbm] * 5,
        out_specs=[hbm] * 5,
        scratch_shapes=[pltpu.VMEM(value.shape, value.dtype) for value in results] + [dma((2, 5))],
        compiler_params=pltpu.CompilerParams(vmem_limit_bytes=VMEM_LIMIT),
    )(*results)


def solution(mesh):
    experts = mesh.shape["expert"]
    side = next(s for s in range(1, experts + 1) if s * s == experts)
    in_specs = (
        P(("expert", "dp"), "pipe"),
        P(("expert", "dp"), "pipe"),
        P(("expert", "dp"), None),
        P(("expert", "dp"), None),
        P("expert", "pipe", None),
        P("expert", "pipe", None),
        P("expert", None, "pipe"),
    )
    out_specs = (
        P(("expert", "dp"), "pipe"),
        P(("expert", "dp"), "pipe"),
        P("expert", "pipe", "dp"),
        P("expert", "pipe", "dp"),
        P("expert", "dp", "pipe"),
    )
    return jax.shard_map(
        functools.partial(on_device, side), mesh=mesh, in_specs=in_specs, out_specs=out_specs, check_vma=False
    )
```

time: 103 us -> 95.6 us (0.928); the launches traced: 103 us -> 94 us
  local copies, waits for them, and re-layouts: 8.83 us -> 0 us
    unnamed x19 -> x0, local copies, waits for them, and re-layouts: 8.83 us -> none
    pallas_call x0 -> x1, Pallas kernels: none -> 2.3 us  [on_device(): pl.pallas_call(store, out_shape=[jax.ShapeDtypeStruct(value.shape, value....]
    pallas_call x1, Pallas kernels: 93.3 us -> 91.1 us  [on_device(): pl.pallas_call(functools.partial(kernel, side), out_shape=(jax.ShapeDtype...]
where the time goes in v2:
time: 95.6 us; the launch traced here: 94 us
  Pallas kernels  93.4 us (98%)
    pallas_call x1, Pallas kernels, on_device(): pl.pallas_call(functools.partial(kernel, side), out_shape=(jax.ShapeDtype...  91.1 us
    pallas_call x1, Pallas kernels, on_device(): pl.pallas_call(store, out_shape=[jax.ShapeDtypeStruct(value.shape, value....  2.3 us

profile of v2, /device:TPU:1, one launch (start us, length us, event | category | flops | bytes accessed | tf_op | source)
XLA Modules:
  0.0 94.0 jit_solution(11923460422422669911)
XLA Ops:
  0.6 91.1 %shard_map.110 = (bf16[16,512]{1,0:T(8,128)(2,1)}, bf16[16,512]{1,0:T(8,128)(2,1)}, bf16[1,512,512]{2,1,0:T(8,128)(2,1)}, bf16[1,512,512]{2,1,0:T(8,128)(2,1)}, bf16[1,512,512]{2,1,0:T(8,128)(2,1)}) custom-call(bf16[16,512]{1,0:T(8,128)(2,1)} %tok_ref.1, bf16[16,512]{1,0:T(8,128)(2,1)} %cot_ref.1, s32[8,16]{1,0:T(8,128)} %bitcast.2, f32[8,16]{1,0:T(8,128)} %bitcast.3, ...), custom_call_target="tpu_custom_call" | custom-call | flops 1610612736 | bytes 3145728 | tf_op jit(solution)/shard_map/pallas_call | solution.py:377
  91.7 2.3 %shard_map.111 = (bf16[16,512]{1,0:T(8,128)(2,1)}, bf16[16,512]{1,0:T(8,128)(2,1)}, bf16[1,512,512]{2,1,0:T(8,128)(2,1)}, bf16[1,512,512]{2,1,0:T(8,128)(2,1)}, bf16[1,512,512]{2,1,0:T(8,128)(2,1)}) custom-call(bf16[16,512]{1,0:T(8,128)(2,1)} %get-tuple-element.10.refs_0_, bf16[16,512]{1,0:T(8,128)(2,1)} %get-tuple-element.11.refs_1_, ...), custom_call_target="tpu_custom_call" | custom-call | tf_op jit(solution)/shard_map/pallas_call | solution.py:439

commit v3 on v2

--- a/solution.py
+++ b/solution.py
@@ -40,8 +40,8 @@
     mixed_out, grad_out, gg_out, gu_out, gd_out,
     routes_vmem, gates_vmem, mixed_ref, grad_ref, gg_ref, gu_ref, gd_ref, in_sem, out_sem, wg, wu, wd,
     tokbuf, metabuf, cmat, perm, perm_back, send2, recv2, x_ref, do_ref, pair_send, pair_recv, mine,
-    far_send, far_recv, imm_send, imm_recv, sum_send, sum_recv, act, send3, recv3, send4, recv4,
-    w_sem, s1, r1, s1m, r1m, s2, r2, sp, rp, sy, ry, s5, r5, s3, r3, s4, r4,
+    far_send, far_recv, imm_send, imm_recv, sum_send, sum_recv, act, send3, recv3, send4, recv4, acc, other,
+    w_sem, s1, r1, s1m, r1m, s2, r2, sp, rp, sy, ry, s5, r5, s3, r3, s4, r4, s6, r6,
 ):
     toks, piece = tok_ref.shape
     top = routes_ref.shape[0]
@@ -49,7 +49,7 @@
     block = side * CAP
     rows = side * block
     size = 2 * rows
-    width = wg.shape[1]
+    width = wg.shape[2]
     cols = width // CHIPS
     part = rows // 4
 
@@ -85,12 +85,17 @@
     ]
     for load in inputs:
         load.start()
-    off = pl.multiple_of(d * width, width)
-    loads = [
-        pltpu.make_async_copy(wg_hbm.at[0, :, pl.ds(off, width)], wg, w_sem.at[0]),
-        pltpu.make_async_copy(wu_hbm.at[0, :, pl.ds(off, width)], wu, w_sem.at[1]),
-        pltpu.make_async_copy(wd_hbm.at[0, pl.ds(off, width), :], wd, w_sem.at[2]),
-    ]
+    loads = []
+    for s in range(2):
+        off = pl.multiple_of((d * s + (1 - d) * (1 - s)) * width, width)
+        for k, (src, dst) in enumerate(
+            (
+                (wg_hbm.at[0, :, pl.ds(off, width)], wg.at[s]),
+                (wu_hbm.at[0, :, pl.ds(off, width)], wu.at[s]),
+                (wd_hbm.at[0, pl.ds(off, width), :], wd.at[s]),
+            )
+        ):
+            loads.append(pltpu.make_async_copy(src, dst, w_sem.at[s, k]))
     for load in loads:
         load.start()
 
@@ -179,28 +184,27 @@
         wide.append(jnp.concatenate([empty, empty, picks[i]], axis=1))
     cmat[...] = jnp.concatenate(wide, axis=0).T.astype(BF16)
 
-    for load in loads:
-        load.wait()
-
     pair, fars, imms, sums, ups, dns, sibs, relays = ([None, None] for _ in range(8))
     ring = ((up, up_dev, dn, dn_dev), (dn, dn_dev, up, up_dev))
 
     def partials(s, core, out, cast):
-        at = pl.ds(pl.multiple_of(s * rows + core * 2 * part, 2 * part), 2 * part)
+        at = pl.ds(pl.multiple_of(core * 2 * part, 2 * part), 2 * part)
         xs, ds = x_ref[at, :], do_ref[at, :]
-        for q, value in enumerate((dot(xs, wg[...]), dot(xs, wu[...]), dot_cols(ds, wd[...]))):
+        for q, value in enumerate((dot(xs, wg[s]), dot(xs, wu[s]), dot_cols(ds, wd[s]))):
             for h in range(2):
                 for k in range(CHIPS):
                     out[s, h, k, q * part : (q + 1) * part, :] = value[
                         h * part : (h + 1) * part, k * cols : (k + 1) * cols
                     ].astype(cast)
 
-    def project(s):
+    def arrange(s):
         for copy in to_experts[s]:
             copy.wait_recv()
         found = dot(perm[...], recv2[s].reshape(size, piece)).astype(BF16)
         x_ref[s * rows : (s + 1) * rows, :] = found[:rows]
         do_ref[s * rows : (s + 1) * rows, :] = found[rows:]
+
+    def project(s):
         partials(s, 1 - c, pair_send, BF16)
         pair[s] = send(pair_send.at[s], pair_recv.at[s], sp.at[s], rp.at[s], sib_dev)
         partials(s, c, mine, F32)
@@ -208,12 +212,14 @@
     def chip_sum(s, h, k):
         return mine[s, h, k] + pair_recv[s, h, k].astype(F32)
 
-    def scatter_start(s):
+    def scatter_far(s):
         fars[s], imms[s] = [], []
         pair[s].wait_recv()
         for h in range(2):
             far_send[s, h] = chip_sum(s, h, far).astype(BF16)
             fars[s].append(send(far_send.at[s, h], far_recv.at[s, h], sy.at[s, h], ry.at[s, h], ring[h][1]))
+
+    def scatter_near(s):
         for h in range(2):
             imm_send[s, h] = chip_sum(s, h, ring[h][2]).astype(BF16)
             imms[s].append(
@@ -230,7 +236,7 @@
             )
 
     def pass_on(s, k, core, h, sem, dev):
-        ref = act.at[s, k, core, h]
+        ref = act.at[s, core, k, h]
         return send(ref, ref, s5.at[s, sem], r5.at[s, sem], dev)
 
     def activate(s):
@@ -241,9 +247,9 @@
             pre = chip_sum(s, h, j) + imm_recv[s, h].astype(F32) + sum_recv[s, h].astype(F32)
             gate, upv, hid_grad = pre[:part], pre[part : 2 * part], pre[2 * part :]
             silu, slope = silu_parts(gate)
-            act[s, j, c, h, 0:part, :] = (silu * upv).astype(BF16)
-            act[s, j, c, h, part : 2 * part, :] = (hid_grad * upv * slope).astype(BF16)
-            act[s, j, c, h, 2 * part :, :] = (hid_grad * silu).astype(BF16)
+            act[s, c, j, h, 0:part, :] = (silu * upv).astype(BF16)
+            act[s, c, j, h, part : 2 * part, :] = (hid_grad * upv * slope).astype(BF16)
+            act[s, c, j, h, 2 * part :, :] = (hid_grad * silu).astype(BF16)
             ups[s].append(pass_on(s, j, c, h, h, up_dev))
             dns[s].append(pass_on(s, j, c, h, 2 + h, dn_dev))
             sibs[s].append(pass_on(s, j, c, h, 6 + h, sib_dev))
@@ -267,63 +273,55 @@
         for copy in sibs[s]:
             copy.wait_recv()
 
-    def gathered(s, q):
+    def gathered(ref, q):
         at = slice(q * part, (q + 1) * part)
         return jnp.concatenate(
             [
-                jnp.concatenate([act[s, k, core, h, at, :] for k in range(CHIPS)], axis=1)
+                jnp.concatenate([ref[core, k, h, at, :] for k in range(CHIPS)], axis=1)
                 for core in range(2)
                 for h in range(2)
             ],
             axis=0,
         )
 
-    to_tokens = [[], []]
-
     def answer(s):
-        outs = dot(gathered(s, 0), wd[...])
-        row_grads = dot_cols(gathered(s, 1), wg[...]) + dot_cols(gathered(s, 2), wu[...])
-        stacked = jnp.concatenate([outs, row_grads], axis=0).astype(BF16)
-        send3[s] = dot(perm_back[...], stacked).astype(BF16).reshape(side, 2 * block, piece)
-        for i in b_peers[s]:
-            to_tokens[s].append(
-                send(send3.at[s, lax.rem(b + i, side)], recv3.at[s, b], s3.at[s, i], r3.at[s, i], b_dev(i, s))
-            )
-        if s == 0:
-            recv3[0, b] = send3[0, b]
-
+        outs = dot(gathered(act.at[s], 0), wd[s])
+        row_grads = dot_cols(gathered(act.at[s], 1), wg[s]) + dot_cols(gathered(act.at[s], 2), wu[s])
+        return outs, row_grads
+
+    arrange(0)
+    for load in loads:
+        load.wait()
     project(0)
-    scatter_start(0)
     project(1)
+    scatter_far(0)
+    scatter_near(0)
+    scatter_far(1)
     scatter_end(0)
-    scatter_start(1)
+    scatter_near(1)
     activate(0)
     scatter_end(1)
     relay(0)
     activate(1)
     relay_end(0)
+    acc[0], acc[1] = answer(0)
     relay(1)
-    answer(0)
+    swap = send(act.at[0, c], other.at[c], s6.at[0], r6.at[0], (p, e, 1 - d))
     relay_end(1)
-    answer(1)
-
-    hidden, gate_grad, up_grad = (
-        jnp.concatenate([gathered(0, q), gathered(1, q)], axis=0) for q in range(3)
-    )
-    stores = []
-    for k, (ref, out, left, right) in enumerate(
-        ((gg_ref, gg_out, x_ref[...], gate_grad), (gu_ref, gu_out, x_ref[...], up_grad), (gd_ref, gd_out, hidden, do_ref[...]))
-    ):
-        ref[...] = dot_rows(left, right).astype(BF16)
-        stores.append(pltpu.make_async_copy(ref, out.at[0], out_sem.at[k]))
-        stores[-1].start()
-
-    both = None
-    for s in range(2):
-        for copy in to_tokens[s]:
-            copy.wait_recv()
-        value = dot(cmat[...], recv3[s].reshape(size, piece))
-        both = value if both is None else both + value
+    outs, row_grads = answer(1)
+    stacked = jnp.concatenate([acc[0] + outs, acc[1] + row_grads], axis=0).astype(BF16)
+    send3[...] = dot(perm_back[...], stacked).astype(BF16).reshape(side, 2 * block, piece)
+    to_tokens = []
+    for i in b_peers[0]:
+        to_tokens.append(send(send3.at[lax.rem(b + i, side)], recv3.at[b], s3.at[i], r3.at[i], b_dev(i, 0)))
+    recv3[b] = send3[b]
+    arrange(1)
+    swap.wait_recv()
+    swap_sib = send(other.at[c], other.at[c], s6.at[1], r6.at[1], sib_dev)
+
+    for copy in to_tokens:
+        copy.wait_recv()
+    both = dot(cmat[...], recv3[...].reshape(size, piece))
     part_mixed = both[:lanes] + both[lanes : 2 * lanes]
     part_grad = both[2 * lanes :]
     for i in range(side):
@@ -333,6 +331,19 @@
     for i in range(1, side):
         home.append(send(send4.at[lax.rem(a + i, side)], recv4.at[a], s4.at[i], r4.at[i], a_dev(i)))
     recv4[a] = send4[a]
+
+    swap_sib.wait_recv()
+    hidden, gate_grad, up_grad = (
+        jnp.concatenate([gathered(act.at[1], q), gathered(other, q)], axis=0) for q in range(3)
+    )
+    stores = []
+    for k, (ref, out, left, right) in enumerate(
+        ((gg_ref, gg_out, x_ref[...], gate_grad), (gu_ref, gu_out, x_ref[...], up_grad), (gd_ref, gd_out, hidden, do_ref[...]))
+    ):
+        ref[...] = dot_rows(left, right).astype(BF16)
+        stores.append(pltpu.make_async_copy(ref, out.at[0], out_sem.at[k]))
+        stores[-1].start()
+
     for copy in home:
         copy.wait_recv()
     final = recv4[0].astype(F32)
@@ -394,9 +405,9 @@
             pltpu.VMEM((piece, width), BF16),
             pltpu.VMEM((width, piece), BF16),
             dma((4,)), dma((5,)),
-            pltpu.VMEM((piece, width), BF16),
-            pltpu.VMEM((piece, width), BF16),
-            pltpu.VMEM((width, piece), BF16),
+            pltpu.VMEM((2, piece, width), BF16),
+            pltpu.VMEM((2, piece, width), BF16),
+            pltpu.VMEM((2, width, piece), BF16),
             pltpu.VMEM((side, 2 * toks, piece), BF16),
             pltpu.VMEM((side, 2 * top, lanes), F32),
             pltpu.VMEM((3 * lanes, 2 * rows), BF16),
@@ -415,19 +426,22 @@
             pltpu.VMEM(halves, BF16),
             pltpu.VMEM(halves, BF16),
             pltpu.VMEM(halves, BF16),
-            pltpu.VMEM((2, CHIPS, 2, 2, 3 * part, width // CHIPS), BF16),
-            pltpu.VMEM((2, side, 2 * block, piece), BF16),
-            pltpu.VMEM((2, side, 2 * block, piece), BF16),
+            pltpu.VMEM((2, 2, CHIPS, 2, 3 * part, width // CHIPS), BF16),
+            pltpu.VMEM((side, 2 * block, piece), BF16),
+            pltpu.VMEM((side, 2 * block, piece), BF16),
             pltpu.VMEM((side, 2 * toks, piece), BF16),
             pltpu.VMEM((side, 2 * toks, piece), BF16),
-            dma((3,)),
+            pltpu.VMEM((2, rows, piece), F32),
+            pltpu.VMEM((2, CHIPS, 2, 3 * part, width // CHIPS), BF16),
+            dma((2, 3)),
             dma((side,)), dma((side,)), dma((side,)), dma((side,)),
             dma((2, side)), dma((2, side)),
             dma((2,)), dma((2,)),
             dma((2, 6)), dma((2, 6)),
             dma((2, 14)), dma((2, 14)),
-            dma((2, side)), dma((2, side)),
             dma((side,)), dma((side,)),
+            dma((side,)), dma((side,)),
+            dma((2,)), dma((2,)),
         ],
         compiler_params=pltpu.CompilerParams(
             collective_id=0, has_side_effects=True, vmem_limit_bytes=VMEM_LIMIT

time: 95.6 us -> 90.6 us (0.948)
  Pallas kernels: 93.4 us -> 89.2 us
    pallas_call x1, Pallas kernels: 91.1 us -> 86.9 us  [on_device(): pl.pallas_call(functools.partial(kernel, side), out_shape=(jax.ShapeDtype...]
where the time goes in v3:
time: 90.6 us; the launch traced here: 89.8 us
  Pallas kernels  89.2 us (98%)
    pallas_call x1, Pallas kernels, on_device(): pl.pallas_call(functools.partial(kernel, side), out_shape=(jax.ShapeDtype...  86.9 us
    pallas_call x1, Pallas kernels, on_device(): pl.pallas_call(store, out_shape=[jax.ShapeDtypeStruct(value.shape, value....  2.3 us

profile of v3, /device:TPU:1, one launch (start us, length us, event | category | flops | bytes accessed | tf_op | source)
XLA Modules:
  0.0 89.8 jit_solution(14331219892641880754)
XLA Ops:
  0.6 86.9 %shard_map.110 = (bf16[16,512]{1,0:T(8,128)(2,1)}, bf16[16,512]{1,0:T(8,128)(2,1)}, bf16[1,512,512]{2,1,0:T(8,128)(2,1)}, bf16[1,512,512]{2,1,0:T(8,128)(2,1)}, bf16[1,512,512]{2,1,0:T(8,128)(2,1)}) custom-call(bf16[16,512]{1,0:T(8,128)(2,1)} %tok_ref.1, bf16[16,512]{1,0:T(8,128)(2,1)} %cot_ref.1, s32[8,16]{1,0:T(8,128)} %bitcast.2, f32[8,16]{1,0:T(8,128)} %bitcast.3, ...), custom_call_target="tpu_custom_call" | custom-call | flops 1610612736 | bytes 3145728 | tf_op jit(solution)/shard_map/pallas_call | solution.py:388
  87.5 2.3 %shard_map.111 = (bf16[16,512]{1,0:T(8,128)(2,1)}, bf16[16,512]{1,0:T(8,128)(2,1)}, bf16[1,512,512]{2,1,0:T(8,128)(2,1)}, bf16[1,512,512]{2,1,0:T(8,128)(2,1)}, bf16[1,512,512]{2,1,0:T(8,128)(2,1)}) custom-call(bf16[16,512]{1,0:T(8,128)(2,1)} %get-tuple-element.10.refs_0_, bf16[16,512]{1,0:T(8,128)(2,1)} %get-tuple-element.11.refs_1_, ...), custom_call_target="tpu_custom_call" | custom-call | tf_op jit(solution)/shard_map/pallas_call | solution.py:453

commit v4 on v3

--- a/solution.py
+++ b/solution.py
@@ -37,11 +37,11 @@
 
 def kernel(
     side, tok_ref, cot_ref, routes_ref, gates_ref, wg_hbm, wu_hbm, wd_hbm,
-    mixed_out, grad_out, gg_out, gu_out, gd_out,
-    routes_vmem, gates_vmem, mixed_ref, grad_ref, gg_ref, gu_ref, gd_ref, in_sem, out_sem, wg, wu, wd,
+    recv4, gg_out, gu_out, gd_out,
+    routes_vmem, gates_vmem, gg_ref, gu_ref, gd_ref, in_sem, out_sem, wg, wu, wd,
     tokbuf, metabuf, cmat, perm, perm_back, send2, recv2, x_ref, do_ref, pair_send, pair_recv, mine,
-    far_send, far_recv, imm_send, imm_recv, sum_send, sum_recv, act, send3, recv3, send4, recv4, acc, other,
-    w_sem, s1, r1, s1m, r1m, s2, r2, sp, rp, sy, ry, s5, r5, s3, r3, s4, r4, s6, r6,
+    far_send, far_recv, imm_send, imm_recv, sum_send, sum_recv, act, send3, recv3, send4, acc, other,
+    w_sem, s1, r1, s1m, r1m, s2, r2, sp, rp, sy, ry, s5, r5, s3, r3, s4, r4, s6, r6, s7, r7,
 ):
     toks, piece = tok_ref.shape
     top = routes_ref.shape[0]
@@ -66,14 +66,14 @@
     def a_dev(i):
         return (p, lax.rem(a + i, side) * sa + b * sb, d)
 
-    def b_dev(i, s):
-        return (p, a * sa + lax.rem(b + i, side) * sb, lax.rem(d + s, 2))
-
-    b_peers = [[i for i in range(side) if i or s] for s in range(2)]
+    def b_dev(i):
+        return (p, a * sa + lax.rem(b + i, side) * sb, d)
+
+    group_dev = (p, e, 1 - d)
 
     barrier = pltpu.get_barrier_semaphore()
-    peers = [a_dev(i) for i in range(1, side)] + [b_dev(i, s) for s in range(2) for i in b_peers[s]]
-    peers += [sib_dev, up_dev, dn_dev]
+    peers = [a_dev(i) for i in range(1, side)] + [b_dev(i) for i in range(1, side)]
+    peers += [sib_dev, up_dev, dn_dev, group_dev]
     for dev in peers:
         pl.semaphore_signal(barrier, inc=1, device_id=dev, device_id_type=MESH)
 
@@ -167,13 +167,10 @@
     for i in range(side):
         at = slice(block * i, block * (i + 1))
         send2[i] = jnp.concatenate([xr[at], dr[at]], axis=0).astype(BF16)
-    to_experts = [[], []]
-    for s in range(2):
-        for i in b_peers[s]:
-            to_experts[s].append(
-                send(send2.at[lax.rem(b + i, side)], recv2.at[s, b], s2.at[s, i], r2.at[s, i], b_dev(i, s))
-            )
-    recv2[0, b] = send2[b]
+    to_experts = []
+    for i in range(1, side):
+        to_experts.append(send(send2.at[lax.rem(b + i, side)], recv2.at[b], s2.at[i], r2.at[i], b_dev(i)))
+    recv2[b] = send2[b]
 
     empty = jnp.zeros((block, lanes), F32)
     wide = []
@@ -197,12 +194,12 @@
                         h * part : (h + 1) * part, k * cols : (k + 1) * cols
                     ].astype(cast)
 
-    def arrange(s):
-        for copy in to_experts[s]:
-            copy.wait_recv()
-        found = dot(perm[...], recv2[s].reshape(size, piece)).astype(BF16)
-        x_ref[s * rows : (s + 1) * rows, :] = found[:rows]
-        do_ref[s * rows : (s + 1) * rows, :] = found[rows:]
+    def to_group(ref, k):
+        quarter = rows // 2
+        return send(
+            ref.at[pl.ds(k % 2 * quarter, quarter)], ref.at[pl.ds(rows + k % 2 * quarter, quarter)],
+            s7.at[k], r7.at[k], group_dev,
+        )
 
     def project(s):
         partials(s, 1 - c, pair_send, BF16)
@@ -289,7 +286,12 @@
         row_grads = dot_cols(gathered(act.at[s], 1), wg[s]) + dot_cols(gathered(act.at[s], 2), wu[s])
         return outs, row_grads
 
-    arrange(0)
+    for copy in to_experts:
+        copy.wait_recv()
+    found = dot(perm[...], recv2[...].reshape(size, piece)).astype(BF16)
+    x_ref[:rows, :] = found[:rows]
+    do_ref[:rows, :] = found[rows:]
+    crossing = [to_group(x_ref, 0)]
     for load in loads:
         load.wait()
     project(0)
@@ -306,16 +308,16 @@
     relay_end(0)
     acc[0], acc[1] = answer(0)
     relay(1)
-    swap = send(act.at[0, c], other.at[c], s6.at[0], r6.at[0], (p, e, 1 - d))
+    swap = send(act.at[0, c], other.at[c], s6.at[0], r6.at[0], group_dev)
+    crossing += [to_group(x_ref, 1), to_group(do_ref, 2), to_group(do_ref, 3)]
     relay_end(1)
     outs, row_grads = answer(1)
     stacked = jnp.concatenate([acc[0] + outs, acc[1] + row_grads], axis=0).astype(BF16)
     send3[...] = dot(perm_back[...], stacked).astype(BF16).reshape(side, 2 * block, piece)
     to_tokens = []
-    for i in b_peers[0]:
-        to_tokens.append(send(send3.at[lax.rem(b + i, side)], recv3.at[b], s3.at[i], r3.at[i], b_dev(i, 0)))
+    for i in range(1, side):
+        to_tokens.append(send(send3.at[lax.rem(b + i, side)], recv3.at[b], s3.at[i], r3.at[i], b_dev(i)))
     recv3[b] = send3[b]
-    arrange(1)
     swap.wait_recv()
     swap_sib = send(other.at[c], other.at[c], s6.at[1], r6.at[1], sib_dev)
 
@@ -330,9 +332,12 @@
     home = []
     for i in range(1, side):
         home.append(send(send4.at[lax.rem(a + i, side)], recv4.at[a], s4.at[i], r4.at[i], a_dev(i)))
-    recv4[a] = send4[a]
+    keep = pltpu.make_async_copy(send4.at[a], recv4.at[a], out_sem.at[3])
+    keep.start()
 
     swap_sib.wait_recv()
+    for copy in crossing:
+        copy.wait_recv()
     hidden, gate_grad, up_grad = (
         jnp.concatenate([gathered(act.at[1], q), gathered(other, q)], axis=0) for q in range(3)
     )
@@ -346,26 +351,29 @@
 
     for copy in home:
         copy.wait_recv()
-    final = recv4[0].astype(F32)
-    for i in range(1, side):
-        final = final + recv4[i].astype(F32)
-    mixed_ref[...] = final[:toks].astype(BF16)
-    grad_ref[...] = final[toks:].astype(BF16)
-    for k, (ref, out) in enumerate(((mixed_ref, mixed_out), (grad_ref, grad_out))):
-        stores.append(pltpu.make_async_copy(ref, out, out_sem.at[3 + k]))
-        stores[-1].start()
+    keep.wait()
     for copy in stores:
         copy.wait()
     for copy in started:
         copy.wait_send()
 
 
-def store(*refs):
-    ins, outs, held, sems = refs[:5], refs[5:10], refs[10:15], refs[15]
-    loads = [pltpu.make_async_copy(ins[i], held[i], sems.at[0, i]) for i in range(5)]
-    stores = [pltpu.make_async_copy(held[i], outs[i], sems.at[1, i]) for i in range(5)]
+def store(toks, parts_hbm, *refs):
+    ins, outs, parts, held, both, sems = refs[:3], refs[3:8], refs[8], refs[9:12], refs[12:14], refs[14]
+    load_parts = pltpu.make_async_copy(parts_hbm, parts, sems.at[0, 3])
+    load_parts.start()
+    loads = [pltpu.make_async_copy(ins[i], held[i], sems.at[0, i]) for i in range(3)]
+    stores = [pltpu.make_async_copy(held[i], outs[2 + i], sems.at[1, i]) for i in range(3)]
     for load in loads:
         load.start()
+    load_parts.wait()
+    final = parts[0].astype(F32)
+    for i in range(1, parts.shape[0]):
+        final = final + parts[i].astype(F32)
+    for i in range(2):
+        both[i][...] = final[i * toks : (i + 1) * toks].astype(BF16)
+        stores.append(pltpu.make_async_copy(both[i], outs[i], sems.at[1, 3 + i]))
+        stores[-1].start()
     for load, copy in zip(loads, stores):
         load.wait()
         copy.start()
@@ -381,26 +389,20 @@
     block = side * CAP
     rows = side * block
     part = rows // 4
+    tokens_out = [jax.ShapeDtypeStruct((toks, piece), BF16)] * 2
+    grads = [jax.ShapeDtypeStruct((1, piece, width), BF16)] * 2 + [jax.ShapeDtypeStruct((1, width, piece), BF16)]
     hbm = pl.BlockSpec(memory_space=pltpu.MemorySpace.HBM)
     dma = pltpu.SemaphoreType.DMA
     halves = (2, 2, 3 * part, width // CHIPS)
     pieces = (2, 2, CHIPS, 3 * part, width // CHIPS)
     results = pl.pallas_call(
         functools.partial(kernel, side),
-        out_shape=(
-            jax.ShapeDtypeStruct((toks, piece), BF16),
-            jax.ShapeDtypeStruct((toks, piece), BF16),
-            jax.ShapeDtypeStruct((1, piece, width), BF16),
-            jax.ShapeDtypeStruct((1, piece, width), BF16),
-            jax.ShapeDtypeStruct((1, width, piece), BF16),
-        ),
+        out_shape=(jax.ShapeDtypeStruct((side, 2 * toks, piece), BF16), *grads),
         in_specs=[hbm] * 7,
-        out_specs=(hbm,) * 5,
+        out_specs=(hbm,) * 4,
         scratch_shapes=[
             pltpu.VMEM((top, toks), jnp.int32),
             pltpu.VMEM((top, toks), F32),
-            pltpu.VMEM((toks, piece), BF16),
-            pltpu.VMEM((toks, piece), BF16),
             pltpu.VMEM((piece, width), BF16),
             pltpu.VMEM((piece, width), BF16),
             pltpu.VMEM((width, piece), BF16),
@@ -414,7 +416,7 @@
             pltpu.VMEM((2 * rows, 2 * rows), BF16),
             pltpu.VMEM((2 * rows, 2 * rows), BF16),
             pltpu.VMEM((side, 2 * block, piece), BF16),
-            pltpu.VMEM((2, side, 2 * block, piece), BF16),
+            pltpu.VMEM((side, 2 * block, piece), BF16),
             pltpu.VMEM((2 * rows, piece), BF16),
             pltpu.VMEM((2 * rows, piece), BF16),
             pltpu.VMEM(pieces, BF16),
@@ -430,18 +432,18 @@
             pltpu.VMEM((side, 2 * block, piece), BF16),
             pltpu.VMEM((side, 2 * block, piece), BF16),
             pltpu.VMEM((side, 2 * toks, piece), BF16),
-            pltpu.VMEM((side, 2 * toks, piece), BF16),
             pltpu.VMEM((2, rows, piece), F32),
             pltpu.VMEM((2, CHIPS, 2, 3 * part, width // CHIPS), BF16),
             dma((2, 3)),
             dma((side,)), dma((side,)), dma((side,)), dma((side,)),
-            dma((2, side)), dma((2, side)),
+            dma((side,)), dma((side,)),
             dma((2,)), dma((2,)),
             dma((2, 6)), dma((2, 6)),
             dma((2, 14)), dma((2, 14)),
             dma((side,)), dma((side,)),
             dma((side,)), dma((side,)),
             dma((2,)), dma((2,)),
+            dma((4,)), dma((4,)),
         ],
         compiler_params=pltpu.CompilerParams(
             collective_id=0, has_side_effects=True, vmem_limit_bytes=VMEM_LIMIT
@@ -451,11 +453,11 @@
         ),
     )(tokens, cotangent, routes.T, gates.T, w_gate, w_up, w_down)
     return pl.pallas_call(
-        store,
-        out_shape=[jax.ShapeDtypeStruct(value.shape, value.dtype) for value in results],
-        in_specs=[hbm] * 5,
+        functools.partial(store, toks),
+        out_shape=[*tokens_out, *grads],
+        in_specs=[hbm] * 4,
         out_specs=[hbm] * 5,
-        scratch_shapes=[pltpu.VMEM(value.shape, value.dtype) for value in results] + [dma((2, 5))],
+        scratch_shapes=[pltpu.VMEM(value.shape, value.dtype) for value in (*results, *tokens_out)] + [dma((2, 5))],
         compiler_params=pltpu.CompilerParams(vmem_limit_bytes=VMEM_LIMIT),
     )(*results)
 

time: 90.6 us -> 86.5 us (0.955)
  Pallas kernels: 89.2 us -> 85.6 us
    pallas_call x1, Pallas kernels: 86.9 us -> 83.3 us  [on_device(): pl.pallas_call(functools.partial(kernel, side), out_shape=(jax.ShapeDtype...]
where the time goes in v4:
time: 86.5 us; the launch traced here: 86.3 us
  Pallas kernels  85.6 us (99%)
    pallas_call x1, Pallas kernels, on_device(): pl.pallas_call(functools.partial(kernel, side), out_shape=(jax.ShapeDtype...  83.3 us
    pallas_call x1, Pallas kernels, on_device(): pl.pallas_call(functools.partial(store, toks), out_shape=[*tokens_out, *g...  2.35 us

profile of v4, /device:TPU:1, one launch (start us, length us, event | category | flops | bytes accessed | tf_op | source)
XLA Modules:
  0.0 86.3 jit_solution(1506775096751812349)
XLA Ops:
  0.6 83.3 %shard_map.110 = (bf16[8,32,512]{2,1,0:T(8,128)(2,1)}, bf16[1,512,512]{2,1,0:T(8,128)(2,1)}, bf16[1,512,512]{2,1,0:T(8,128)(2,1)}, bf16[1,512,512]{2,1,0:T(8,128)(2,1)}) custom-call(bf16[16,512]{1,0:T(8,128)(2,1)} %tok_ref.1, bf16[16,512]{1,0:T(8,128)(2,1)} %cot_ref.1, s32[8,16]{1,0:T(8,128)} %bitcast.2, f32[8,16]{1,0:T(8,128)} %bitcast.3, ...), custom_call_target="tpu_custom_call" | custom-call | flops 1610612736 | bytes 3145728 | tf_op jit(solution)/shard_map/pallas_call | solution.py:398
  83.9 2.4 %shard_map.111 = (bf16[16,512]{1,0:T(8,128)(2,1)}, bf16[16,512]{1,0:T(8,128)(2,1)}, bf16[1,512,512]{2,1,0:T(8,128)(2,1)}, bf16[1,512,512]{2,1,0:T(8,128)(2,1)}, bf16[1,512,512]{2,1,0:T(8,128)(2,1)}) custom-call(bf16[8,32,512]{2,1,0:T(8,128)(2,1)} %get-tuple-element.9.parts_hbm, bf16[1,512,512]{2,1,0:T(8,128)(2,1)} %get-tuple-element.10.refs_0_, ...), custom_call_target="tpu_custom_call" | custom-call | tf_op jit(solution)/shard_map/pallas_call | solution.py:455

commit v5 on v4

--- a/solution.py
+++ b/solution.py
@@ -52,6 +52,8 @@
     width = wg.shape[2]
     cols = width // CHIPS
     part = rows // 4
+    feat = piece // 2
+    halves = [slice(f * feat, (f + 1) * feat) for f in range(2)]
 
     p, e, d = lax.axis_index("pipe"), lax.axis_index("expert"), lax.axis_index("dp")
     c, j = lax.rem(p, 2), lax.div(p, 2)
@@ -80,9 +82,14 @@
     inputs = [
         pltpu.make_async_copy(routes_ref, routes_vmem, in_sem.at[0]),
         pltpu.make_async_copy(gates_ref, gates_vmem, in_sem.at[1]),
-        pltpu.make_async_copy(tok_ref, tokbuf.at[a, pl.ds(0, toks)], in_sem.at[2]),
-        pltpu.make_async_copy(cot_ref, tokbuf.at[a, pl.ds(toks, toks)], in_sem.at[3]),
     ]
+    for f in range(2):
+        for k, ref in enumerate((tok_ref, cot_ref)):
+            inputs.append(
+                pltpu.make_async_copy(
+                    ref.at[:, pl.ds(f * feat, feat)], tokbuf.at[f, a, pl.ds(k * toks, toks)], in_sem.at[2 + 2 * f + k]
+                )
+            )
     for load in inputs:
         load.start()
     loads = []
@@ -120,8 +127,9 @@
     gather = []
     for i in range(1, side):
         gather.append(send(metabuf.at[a], metabuf.at[a], s1m.at[i], r1m.at[i], a_dev(i)))
-    for i in range(1, side):
-        gather.append(send(tokbuf.at[a], tokbuf.at[a], s1.at[i], r1.at[i], a_dev(i)))
+    for f in range(2):
+        for i in range(1, side):
+            gather.append(send(tokbuf.at[f, a], tokbuf.at[f, a], s1.at[f, i], r1.at[f, i], a_dev(i)))
 
     def sorted_place(at):
         at_b, at = lax.div(at, 2 * block), lax.rem(at, 2 * block)
@@ -160,17 +168,20 @@
     place = jnp.concatenate(picks, axis=0).astype(BF16)
     scale = jnp.concatenate(scales, axis=0)
 
-    for copy in gather[side - 1 :]:
-        copy.wait_recv()
-    xr = dot(place, tokbuf[:, 0:toks, :].reshape(lanes, piece))
-    dr = dot(place, tokbuf[:, toks:, :].reshape(lanes, piece)) * scale
-    for i in range(side):
-        at = slice(block * i, block * (i + 1))
-        send2[i] = jnp.concatenate([xr[at], dr[at]], axis=0).astype(BF16)
     to_experts = []
-    for i in range(1, side):
-        to_experts.append(send(send2.at[lax.rem(b + i, side)], recv2.at[b], s2.at[i], r2.at[i], b_dev(i)))
-    recv2[b] = send2[b]
+    for f in range(2):
+        for copy in gather[(f + 1) * (side - 1) : (f + 2) * (side - 1)]:
+            copy.wait_recv()
+        xr = dot(place, tokbuf[f, :, 0:toks, :].reshape(lanes, feat))
+        dr = dot(place, tokbuf[f, :, toks:, :].reshape(lanes, feat)) * scale
+        for i in range(side):
+            at = slice(block * i, block * (i + 1))
+            send2[f, i] = jnp.concatenate([xr[at], dr[at]], axis=0).astype(BF16)
+        for i in range(1, side):
+            to_experts.append(
+                send(send2.at[f, lax.rem(b + i, side)], recv2.at[f, b], s2.at[f, i], r2.at[f, i], b_dev(i))
+            )
+        recv2[f, b] = send2[f, b]
 
     empty = jnp.zeros((block, lanes), F32)
     wide = []
@@ -281,16 +292,12 @@
             axis=0,
         )
 
-    def answer(s):
-        outs = dot(gathered(act.at[s], 0), wd[s])
-        row_grads = dot_cols(gathered(act.at[s], 1), wg[s]) + dot_cols(gathered(act.at[s], 2), wu[s])
-        return outs, row_grads
-
     for copy in to_experts:
         copy.wait_recv()
-    found = dot(perm[...], recv2[...].reshape(size, piece)).astype(BF16)
-    x_ref[:rows, :] = found[:rows]
-    do_ref[:rows, :] = found[rows:]
+    for f, at in enumerate(halves):
+        found = dot(perm[...], recv2[f].reshape(size, feat)).astype(BF16)
+        x_ref[:rows, at] = found[:rows]
+        do_ref[:rows, at] = found[rows:]
     crossing = [to_group(x_ref, 0)]
     for load in loads:
         load.wait()
@@ -306,40 +313,50 @@
     relay(0)
     activate(1)
     relay_end(0)
-    acc[0], acc[1] = answer(0)
+    acc[0] = dot(gathered(act.at[0], 0), wd[0])
+    acc[1] = dot_cols(gathered(act.at[0], 1), wg[0]) + dot_cols(gathered(act.at[0], 2), wu[0])
     relay(1)
     swap = send(act.at[0, c], other.at[c], s6.at[0], r6.at[0], group_dev)
     crossing += [to_group(x_ref, 1), to_group(do_ref, 2), to_group(do_ref, 3)]
     relay_end(1)
-    outs, row_grads = answer(1)
-    stacked = jnp.concatenate([acc[0] + outs, acc[1] + row_grads], axis=0).astype(BF16)
-    send3[...] = dot(perm_back[...], stacked).astype(BF16).reshape(side, 2 * block, piece)
+    hidden, gate_grad, up_grad = (gathered(act.at[1], q) for q in range(3))
     to_tokens = []
-    for i in range(1, side):
-        to_tokens.append(send(send3.at[lax.rem(b + i, side)], recv3.at[b], s3.at[i], r3.at[i], b_dev(i)))
-    recv3[b] = send3[b]
+    for f, at in enumerate(halves):
+        outs = acc[0, :, at] + dot(hidden, wd[1, :, at])
+        row_grads = acc[1, :, at] + dot_cols(gate_grad, wg[1, at, :]) + dot_cols(up_grad, wu[1, at, :])
+        stacked = jnp.concatenate([outs, row_grads], axis=0).astype(BF16)
+        send3[f] = dot(perm_back[...], stacked).astype(BF16).reshape(side, 2 * block, feat)
+        for i in range(1, side):
+            to_tokens.append(
+                send(send3.at[f, lax.rem(b + i, side)], recv3.at[f, b], s3.at[f, i], r3.at[f, i], b_dev(i))
+            )
+        recv3[f, b] = send3[f, b]
     swap.wait_recv()
     swap_sib = send(other.at[c], other.at[c], s6.at[1], r6.at[1], sib_dev)
 
-    for copy in to_tokens:
-        copy.wait_recv()
-    both = dot(cmat[...], recv3[...].reshape(size, piece))
-    part_mixed = both[:lanes] + both[lanes : 2 * lanes]
-    part_grad = both[2 * lanes :]
-    for i in range(side):
-        at = slice(i * toks, (i + 1) * toks)
-        send4[i] = jnp.concatenate([part_mixed[at], part_grad[at]], axis=0).astype(BF16)
     home = []
-    for i in range(1, side):
-        home.append(send(send4.at[lax.rem(a + i, side)], recv4.at[a], s4.at[i], r4.at[i], a_dev(i)))
-    keep = pltpu.make_async_copy(send4.at[a], recv4.at[a], out_sem.at[3])
-    keep.start()
+    for f in range(2):
+        for copy in to_tokens[f * (side - 1) : (f + 1) * (side - 1)]:
+            copy.wait_recv()
+        both = dot(cmat[...], recv3[f].reshape(size, feat))
+        part_mixed = both[:lanes] + both[lanes : 2 * lanes]
+        part_grad = both[2 * lanes :]
+        for i in range(side):
+            at = slice(i * toks, (i + 1) * toks)
+            send4[f, i] = jnp.concatenate([part_mixed[at], part_grad[at]], axis=0).astype(BF16)
+        for i in range(1, side):
+            home.append(
+                send(send4.at[f, lax.rem(a + i, side)], recv4.at[f, a], s4.at[f, i], r4.at[f, i], a_dev(i))
+            )
+        home.append(pltpu.make_async_copy(send4.at[f, a], recv4.at[f, a], out_sem.at[3 + f]))
+        home[-1].start()
 
     swap_sib.wait_recv()
     for copy in crossing:
         copy.wait_recv()
     hidden, gate_grad, up_grad = (
-        jnp.concatenate([gathered(act.at[1], q), gathered(other, q)], axis=0) for q in range(3)
+        jnp.concatenate([mine_q, gathered(other, q)], axis=0)
+        for q, mine_q in enumerate((hidden, gate_grad, up_grad))
     )
     stores = []
     for k, (ref, out, left, right) in enumerate(
@@ -349,9 +366,11 @@
         stores.append(pltpu.make_async_copy(ref, out.at[0], out_sem.at[k]))
         stores[-1].start()
 
-    for copy in home:
-        copy.wait_recv()
-    keep.wait()
+    for copy in home[side - 1 :: side]:
+        copy.wait()
+    for f in range(2):
+        for copy in home[f * side : f * side + side - 1]:
+            copy.wait_recv()
     for copy in stores:
         copy.wait()
     for copy in started:
@@ -367,9 +386,10 @@
     for load in loads:
         load.start()
     load_parts.wait()
-    final = parts[0].astype(F32)
-    for i in range(1, parts.shape[0]):
-        final = final + parts[i].astype(F32)
+    final = parts[:, 0].astype(F32)
+    for i in range(1, parts.shape[1]):
+        final = final + parts[:, i].astype(F32)
+    final = jnp.concatenate([final[0], final[1]], axis=1)
     for i in range(2):
         both[i][...] = final[i * toks : (i + 1) * toks].astype(BF16)
         stores.append(pltpu.make_async_copy(both[i], outs[i], sems.at[1, 3 + i]))
@@ -393,11 +413,12 @@
     grads = [jax.ShapeDtypeStruct((1, piece, width), BF16)] * 2 + [jax.ShapeDtypeStruct((1, width, piece), BF16)]
     hbm = pl.BlockSpec(memory_space=pltpu.MemorySpace.HBM)
     dma = pltpu.SemaphoreType.DMA
+    feat = piece // 2
     halves = (2, 2, 3 * part, width // CHIPS)
     pieces = (2, 2, CHIPS, 3 * part, width // CHIPS)
     results = pl.pallas_call(
         functools.partial(kernel, side),
-        out_shape=(jax.ShapeDtypeStruct((side, 2 * toks, piece), BF16), *grads),
+        out_shape=(jax.ShapeDtypeStruct((2, side, 2 * toks, feat), BF16), *grads),
         in_specs=[hbm] * 7,
         out_specs=(hbm,) * 4,
         scratch_shapes=[
@@ -406,17 +427,17 @@
             pltpu.VMEM((piece, width), BF16),
             pltpu.VMEM((piece, width), BF16),
             pltpu.VMEM((width, piece), BF16),
-            dma((4,)), dma((5,)),
+            dma((6,)), dma((5,)),
             pltpu.VMEM((2, piece, width), BF16),
             pltpu.VMEM((2, piece, width), BF16),
             pltpu.VMEM((2, width, piece), BF16),
-            pltpu.VMEM((side, 2 * toks, piece), BF16),
+            pltpu.VMEM((2, side, 2 * toks, feat), BF16),
             pltpu.VMEM((side, 2 * top, lanes), F32),
             pltpu.VMEM((3 * lanes, 2 * rows), BF16),
             pltpu.VMEM((2 * rows, 2 * rows), BF16),
             pltpu.VMEM((2 * rows, 2 * rows), BF16),
-            pltpu.VMEM((side, 2 * block, piece), BF16),
-            pltpu.VMEM((side, 2 * block, piece), BF16),
+            pltpu.VMEM((2, side, 2 * block, feat), BF16),
+            pltpu.VMEM((2, side, 2 * block, feat), BF16),
             pltpu.VMEM((2 * rows, piece), BF16),
             pltpu.VMEM((2 * rows, piece), BF16),
             pltpu.VMEM(pieces, BF16),
@@ -429,19 +450,19 @@
             pltpu.VMEM(halves, BF16),
             pltpu.VMEM(halves, BF16),
             pltpu.VMEM((2, 2, CHIPS, 2, 3 * part, width // CHIPS), BF16),
-            pltpu.VMEM((side, 2 * block, piece), BF16),
-            pltpu.VMEM((side, 2 * block, piece), BF16),
-            pltpu.VMEM((side, 2 * toks, piece), BF16),
+            pltpu.VMEM((2, side, 2 * block, feat), BF16),
+            pltpu.VMEM((2, side, 2 * block, feat), BF16),
+            pltpu.VMEM((2, side, 2 * toks, feat), BF16),
             pltpu.VMEM((2, rows, piece), F32),
             pltpu.VMEM((2, CHIPS, 2, 3 * part, width // CHIPS), BF16),
             dma((2, 3)),
-            dma((side,)), dma((side,)), dma((side,)), dma((side,)),
-            dma((side,)), dma((side,)),
+            dma((2, side)), dma((2, side)), dma((side,)), dma((side,)),
+            dma((2, side)), dma((2, side)),
             dma((2,)), dma((2,)),
             dma((2, 6)), dma((2, 6)),
             dma((2, 14)), dma((2, 14)),
-            dma((side,)), dma((side,)),
-            dma((side,)), dma((side,)),
+            dma((2, side)), dma((2, side)),
+            dma((2, side)), dma((2, side)),
             dma((2,)), dma((2,)),
             dma((4,)), dma((4,)),
         ],

time: 86.5 us -> 85.9 us (level)
  no operation moved by 1% of the time
where the time goes in v5:
time: 85.9 us; the launch traced here: 85.7 us
  Pallas kernels  85.1 us (99%)
    pallas_call x1, Pallas kernels, on_device(): pl.pallas_call(functools.partial(kernel, side), out_shape=(jax.ShapeDtype...  82.7 us
    pallas_call x1, Pallas kernels, on_device(): pl.pallas_call(functools.partial(store, toks), out_shape=[*tokens_out, *g...  2.35 us

profile of v5, /device:TPU:1, one launch (start us, length us, event | category | flops | bytes accessed | tf_op | source)
XLA Modules:
  0.0 85.7 jit_solution(14495959785131684111)
XLA Ops:
  0.6 82.7 %shard_map.110 = (bf16[2,8,32,256]{3,2,1,0:T(8,128)(2,1)}, bf16[1,512,512]{2,1,0:T(8,128)(2,1)}, bf16[1,512,512]{2,1,0:T(8,128)(2,1)}, bf16[1,512,512]{2,1,0:T(8,128)(2,1)}) custom-call(bf16[16,512]{1,0:T(8,128)(2,1)} %tok_ref.1, bf16[16,512]{1,0:T(8,128)(2,1)} %cot_ref.1, s32[8,16]{1,0:T(8,128)} %bitcast.2, f32[8,16]{1,0:T(8,128)} %bitcast.3, ...), custom_call_target="tpu_custom_call" | custom-call | flops 1610612736 | bytes 3145728 | tf_op jit(solution)/shard_map/pallas_call | solution.py:419
  83.3 2.4 %shard_map.111 = (bf16[16,512]{1,0:T(8,128)(2,1)}, bf16[16,512]{1,0:T(8,128)(2,1)}, bf16[1,512,512]{2,1,0:T(8,128)(2,1)}, bf16[1,512,512]{2,1,0:T(8,128)(2,1)}, bf16[1,512,512]{2,1,0:T(8,128)(2,1)}) custom-call(bf16[2,8,32,256]{3,2,1,0:T(8,128)(2,1)} %get-tuple-element.9.parts_hbm, bf16[1,512,512]{2,1,0:T(8,128)(2,1)} %get-tuple-element.10.refs_0_, ...), custom_call_target="tpu_custom_call" | custom-call | tf_op jit(solution)/shard_map/pallas_call | solution.py:476
